TPU v7x, 128 devices: a whole 4x4x4 slice. The times are simulated.
128 devices in a mesh: stream: 32 (over y, z, core), span: 4 (over x).
Axes of the slice: x: 4, y: 4, z: 4, core: 2. Of those that a mesh axis runs over, the one named last changes fastest.
Arguments:
- right_side: float32 [256, 4, 64, 512], P('stream', None, None, 'span'), may hold values from -6 to 6
- shift_fine: float32 [256, 64, 512], P('stream', None, 'span'), may hold values from 3 to 9
- diag_blocks: bfloat16 [256, 64, 64, 512], P('stream', None, None, 'span'), may hold values from -0.375 to 0.375
- smoother: bfloat16 [256, 64, 64, 512], P('stream', None, None, 'span'), may hold values from -0.09375 to 0.09375
- couplings: bfloat16 [8, 64, 64], replicated, may hold values from -0.25 to 0.25
- coefficients: float32 [8, 256, 512], P(None, 'stream', 'span'), may hold values from 0.5 to 1.5
- agg_ids: int32 [256, 512], P('stream', 'span'), may hold values from 0 to 31, as said below
- coarse_columns: int32 [32, 4, 32, 5], P('stream', 'span'), may hold values from 0 to 31, as said below
- coarse_blocks: float32 [32, 4, 32, 5, 4096], P('stream', 'span'), may hold values from -0.125 to 0.125
- coarse_shift: float32 [32, 4, 32, 64], P('stream', 'span'), may hold values from 2 to 5
Outputs:
- solution: float32 [256, 4, 64, 512], P('stream', None, None, 'span')
Inputs may be any that keep to these rules, and one draw needn't show every extreme that they name: `agg_ids`: within a block of 8 node rows and 128 spanwise nodes, local row s is split into 2 to 4 runs of consecutive spanwise nodes, and the k-th run holds id s * 4 + k; the last local row of every block has 4 runs. `coarse_columns`: index k of a coarse row names an id present in block n_k; at either streamwise end the missing neighbour is replaced by the block itself.
All inputs are finite; a program needn't handle non-finite values.
Results may differ from a plain program's by a relative error of at most 0.004.
Values may be sent and summed in bfloat16 or wider, within the bound.
A program may use at most 256 MiB of HBM per device.

v0:
```python
import jax
import jax.numpy as jnp
from jax import lax
from jax.sharding import PartitionSpec as P

VARS = 64
NRHS = 4
NNZ = 5
CHEB = 8
SWEEPS = 2
AGG_DEV = 32


OMEGA = 0.3
OFFSETS = ((-2, 0), (-1, 0), (1, 0), (2, 0), (0, -2), (0, -1), (0, 1), (0, 2))
PRECISE = lax.Precision.HIGHEST


def padded_2(cells, sides, width):
    for axis, dim in sides:
        count = lax.axis_size(axis)
        head = lax.slice_in_dim(cells, 0, width, axis=dim)
        tail = lax.slice_in_dim(cells, cells.shape[dim] - width, cells.shape[dim], axis=dim)
        cells = jnp.concatenate(
            [
                lax.ppermute(tail, axis, [(i, (i + 1) % count) for i in range(count)]),
                cells,
                lax.ppermute(head, axis, [((i + 1) % count, i) for i in range(count)]),
            ],
            axis=dim,
        )
    return cells


def stream_speed(positions, extent):
    return jnp.sqrt(1.0 + 8.0 * (positions.astype(jnp.float32) + 0.5) / extent)


def block_product(blocks, operand):
    return jnp.einsum("sabp,svbp->svap", blocks, operand, preferred_element_type=jnp.float32)


def clear_ends(padded, margin):
    position = lax.axis_index("stream")
    final_index = lax.axis_size("stream") - 1
    row_index = jnp.arange(padded.shape[0])
    dropped = jnp.logical_or(
        jnp.logical_and(row_index < margin, position == 0),
        jnp.logical_and(row_index >= padded.shape[0] - margin, position == final_index),
    )
    mask_shape = (padded.shape[0],) + (1,) * (padded.ndim - 1)
    return jnp.where(dropped.reshape(mask_shape), jnp.zeros_like(padded), padded)


def apply_padded(padded, shift_fine, diag_blocks, couplings, coefficients, node_speed):
    stream_count = padded.shape[0] - 4
    span_count = padded.shape[3] - 4
    center = padded[2 : stream_count + 2, :, :, 2 : span_count + 2]
    result = shift_fine[:, None, :, :] * center.astype(jnp.float32) + block_product(
        diag_blocks, center
    )
    coupled = jnp.zeros(result.shape, jnp.float32)
    for number in range(8):
        step_stream, step_span = OFFSETS[number]
        shifted = padded[
            2 + step_stream : 2 + step_stream + stream_count,
            :,
            :,
            2 + step_span : 2 + step_span + span_count,
        ]
        product_term = jnp.einsum(
            "ab,svbp->svap", couplings[number], shifted, preferred_element_type=jnp.float32
        )
        coupled = coupled + coefficients[number][:, None, None, :] * product_term
    return result + node_speed[:, None, None, None] * coupled


def smooth(residual, shift_fine, smoother):
    return residual / shift_fine[:, None, :, :] + block_product(
        smoother, residual.astype(jnp.bfloat16)
    )


def selection_tables(columns):
    return (columns[:, :, :, None] == jnp.arange(AGG_DEV)[None, None, None, :]).astype(jnp.float32)


def coarse_apply(neighbors, current, selection, blocks, shifts, live_slots, coarse_speed):
    span_count = current.shape[0]
    row_shape = (span_count, AGG_DEV, NRHS, VARS)
    coupled = jnp.zeros(row_shape, jnp.float32)
    for number in range(NNZ):
        picked = jnp.einsum(
            "qgh,qhz->qgz", selection[:, :, number], neighbors[number], precision=PRECISE
        ).reshape(row_shape)
        coupled = coupled + jnp.einsum(
            "qgab,qgvb->qgva", blocks[:, :, number], picked, precision=PRECISE
        )
    result = shifts[:, :, None, :] * current.reshape(row_shape) + coarse_speed * coupled
    return (live_slots[:, :, None, None] * result).reshape(current.shape)


def row_bound(blocks, shifts, live_slots, coarse_speed):
    absolute = jnp.sum(jnp.abs(blocks), axis=(2, 4))
    return jnp.max(live_slots[:, :, None] * (shifts + coarse_speed * absolute))


def chebyshev(matvec, coarse_rhs, upper_bound):
    upper_edge = 1.05 * upper_bound
    lower_edge = upper_edge / 20.0
    middle = 0.5 * (upper_edge + lower_edge)
    spread = 0.5 * (upper_edge - lower_edge)
    ratio_sigma = middle / spread
    rho_now = 1.0 / ratio_sigma
    iterate = jnp.zeros_like(coarse_rhs)
    remainder = coarse_rhs
    direction = coarse_rhs / middle
    for number in range(CHEB):
        iterate = iterate + direction
        if number + 1 < CHEB:
            remainder = remainder - matvec(direction)
            rho_next = 1.0 / (2.0 * ratio_sigma - rho_now)
            direction = rho_next * rho_now * direction + 2.0 * rho_next / spread * remainder
            rho_now = rho_next
    return iterate


def local(
    right_side,
    shift_fine,
    diag_blocks,
    smoother,
    couplings,
    coefficients,
    agg_ids,
    coarse_columns,
    coarse_blocks,
    coarse_shift,
):
    stream_rows = right_side.shape[0]
    span_nodes = right_side.shape[3]
    node_speed = stream_speed(
        lax.axis_index("stream") * stream_rows + jnp.arange(stream_rows),
        lax.axis_size("stream") * stream_rows,
    )

    def apply_field(vector_field):
        rounded = vector_field.astype(jnp.bfloat16)
        padded = clear_ends(padded_2(rounded, (("stream", 0), ("span", 3)), 2), 2)
        return apply_padded(padded, shift_fine, diag_blocks, couplings, coefficients, node_speed)

    solution = jnp.zeros(right_side.shape, jnp.float32)
    for repeat in range(SWEEPS):
        if repeat == 0:
            residual = right_side
        else:
            residual = right_side - apply_field(solution)
        solution = solution + OMEGA * smooth(residual, shift_fine, smoother)
    residual = right_side - apply_field(solution)
    members = (agg_ids[:, :, None] == jnp.arange(AGG_DEV)[None, None, :]).astype(jnp.float32)
    coarse_rhs = jnp.einsum("spg,svap->gva", members, residual, precision=PRECISE).reshape(
        1, 1, AGG_DEV, NRHS * VARS
    )
    live_slots = (jnp.sum(members, axis=(0, 1)) > 0.0).astype(jnp.float32)
    coarse_speed = stream_speed(lax.axis_index("stream"), lax.axis_size("stream"))
    own_blocks = coarse_blocks.reshape(1, AGG_DEV, NNZ, VARS, VARS)
    own_selection = selection_tables(coarse_columns[0])
    own_shift = coarse_shift[0]
    own_live = live_slots[None, :]
    upper_bound = lax.pmax(
        row_bound(own_blocks, own_shift, own_live, coarse_speed), ("stream", "span")
    )

    def matvec(direction):
        padded = clear_ends(padded_2(direction, (("stream", 0), ("span", 1)), 1), 1)
        neighbors = (padded[1, 1:2], padded[0, 1:2], padded[2, 1:2], padded[1, 0:1], padded[1, 2:3])
        return coarse_apply(
            neighbors, direction[0], own_selection, own_blocks, own_shift, own_live, coarse_speed
        )[None]

    coarse_solution = chebyshev(matvec, coarse_rhs, upper_bound)
    solution_rows = coarse_solution.reshape(AGG_DEV, NRHS * VARS)
    prolonged = jnp.einsum("spg,gz->szp", members, solution_rows, precision=PRECISE).reshape(
        stream_rows, NRHS, VARS, span_nodes
    )
    image_field = apply_field(prolonged)
    solution = solution + prolonged - OMEGA * smooth(image_field, shift_fine, smoother)
    for repeat in range(SWEEPS):
        residual = right_side - apply_field(solution)
        solution = solution + OMEGA * smooth(residual, shift_fine, smoother)
    return solution


def solution(mesh):
    return jax.shard_map(
        local,
        mesh=mesh,
        in_specs=(
            P("stream", None, None, "span"),
            P("stream", None, "span"),
            P("stream", None, None, "span"),
            P("stream", None, None, "span"),
            P(),
            P(None, "stream", "span"),
            P("stream", "span"),
            P("stream", "span", None, None),
            P("stream", "span", None, None, None),
            P("stream", "span", None, None),
        ),
        out_specs=P("stream", None, None, "span"),
        check_vma=False,
    )
```

profile of v0, /device:TPU:0, one launch (start us, length us, event | category | flops | bytes accessed | tf_op | source)
XLA Modules:
  0.0 695.4 jit_solution(15178703669774787825)
XLA Ops:
  0.0 24.1 %copy.823 = bf16[8,64,64,128]{2,1,3,0:T(8,128)(2,1)} copy(bf16[8,64,64,128]{3,2,1,0:T(8,128)(2,1)} %param.13) | data formatting | bytes 16777216 | tf_op args[3]
  25.6 12.4 %fusion.428 = f32[8,128,4,64]{3,2,1,0:T(4,128)S(1)} fusion(bf16[8,4,64,128]{2,1,3,0:T(4,128)(2,1)} %copy.822, bf16[8,64,64,128]{2,1,3,0:T(8,128)(2,1)} %copy.823), kind=kOutput, calls=%fused_computation.595 | convolution fusion | flops 33554432 | bytes 9961472 | tf_op jit(solution)/shard_map/sabp,svbp->svap/dot_general | solution.py:40
  41.2 6.1 collective-permute-start.1
  59.6 24.0 %copy.830 = bf16[8,64,64,128]{2,1,3,0:T(8,128)(2,1)} copy(bf16[8,64,64,128]{3,2,1,0:T(8,128)(2,1)} %param.12) | data formatting | bytes 16777216 | tf_op args[2]
  102.6 13.4 %fusion.429 = f32[8,128,4,64]{3,2,1,0:T(4,128)} fusion(bf16[8,4,64,128]{2,1,3,0:T(4,128)(2,1)} %copy.829, bf16[8,64,64,128]{2,1,3,0:T(8,128)(2,1)} %copy.830), kind=kOutput, calls=%fused_computation.596 | convolution fusion | flops 33554432 | bytes 9961472 | tf_op jit(solution)/shard_map/sabp,svbp->svap/dot_general | solution.py:40
  118.7 5.3 fusion.424
  125.4 12.4 %fusion.430 = f32[8,128,4,64]{3,2,1,0:T(4,128)S(1)} fusion(bf16[8,4,64,128]{2,1,3,0:T(4,128)(2,1)} %copy.832, bf16[8,64,64,128]{2,1,3,0:T(8,128)(2,1)} %copy.823), kind=kOutput, calls=%fused_computation.597 | convolution fusion | flops 33554432 | bytes 9961472 | tf_op jit(solution)/shard_map/sabp,svbp->svap/dot_general | solution.py:40
  143.2 5.1 collective-permute-start.5
  158.7 63.8 %pmax.7 = f32[]{:T(128)} all-reduce(f32[]{:T(128)} %fusion.312), channel_id=1, replica_groups=mesh['stream'=32,'span'=4] {'stream','span'}, use_global_device_ids=true, to_apply=%region_4.5 | all-reduce | flops 1 | bytes 8 | tf_op jit(solution)/shard_map/pmax | solution.py:170
  241.7 13.4 %fusion.431 = f32[8,128,4,64]{3,2,1,0:T(4,128)} fusion(bf16[8,4,64,128]{2,1,3,0:T(4,128)(2,1)} %copy.839, bf16[8,64,64,128]{2,1,3,0:T(8,128)(2,1)} %copy.830), kind=kOutput, calls=%fused_computation.598 | convolution fusion | flops 33554432 | bytes 9961472 | tf_op jit(solution)/shard_map/sabp,svbp->svap/dot_general | solution.py:40
  257.8 3.8 fusion.35
  263.1 5.5 reshape.1312
  268.7 5.1 collective-permute-start.9
  298.9 5.1 collective-permute-start.13
  328.1 5.1 collective-permute-start.17
  357.9 5.1 collective-permute-start.21
  387.6 5.1 collective-permute-start.25
  417.7 5.1 collective-permute-start.29
  447.5 5.1 collective-permute-start.33
  478.7 5.1 collective-permute-start.37
  510.5 13.4 %fusion.432 = f32[8,128,4,64]{3,2,1,0:T(4,128)} fusion(bf16[8,4,64,128]{2,1,3,0:T(4,128)(2,1)} %copy.967, bf16[8,64,64,128]{2,1,3,0:T(8,128)(2,1)} %copy.830), kind=kOutput, calls=%fused_computation.599 | convolution fusion | flops 33554432 | bytes 9961472 | tf_op jit(solution)/shard_map/sabp,svbp->svap/dot_general | solution.py:40
  526.6 5.2 fusion.425
  533.2 12.4 %fusion.433 = f32[8,128,4,64]{3,2,1,0:T(4,128)S(1)} fusion(bf16[8,4,64,128]{2,1,3,0:T(4,128)(2,1)} %copy.970, bf16[8,64,64,128]{2,1,3,0:T(8,128)(2,1)} %copy.823), kind=kOutput, calls=%fused_computation.600 | convolution fusion | flops 33554432 | bytes 9961472 | tf_op jit(solution)/shard_map/sabp,svbp->svap/dot_general | solution.py:40
  547.3 3.7 fusion.404
  551.1 5.1 collective-permute-start.41
  583.8 13.4 %fusion.434 = f32[8,128,4,64]{3,2,1,0:T(4,128)} fusion(bf16[8,4,64,128]{2,1,3,0:T(4,128)(2,1)} %copy.977, bf16[8,64,64,128]{2,1,3,0:T(8,128)(2,1)} %copy.830), kind=kOutput, calls=%fused_computation.601 | convolution fusion | flops 33554432 | bytes 9961472 | tf_op jit(solution)/shard_map/sabp,svbp->svap/dot_general | solution.py:40
  599.9 5.3 fusion.426
  606.6 12.4 %fusion.435 = f32[8,128,4,64]{3,2,1,0:T(4,128)S(1)} fusion(bf16[8,4,64,128]{2,1,3,0:T(4,128)(2,1)} %copy.980, bf16[8,64,64,128]{2,1,3,0:T(8,128)(2,1)} %copy.823), kind=kOutput, calls=%fused_computation.602 | convolution fusion | flops 33554432 | bytes 9961472 | tf_op jit(solution)/shard_map/sabp,svbp->svap/dot_general | solution.py:40
  624.0 5.2 collective-permute-start.45
  656.4 13.4 %fusion.436 = f32[8,128,4,64]{3,2,1,0:T(4,128)} fusion(bf16[8,4,64,128]{2,1,3,0:T(4,128)(2,1)} %copy.987, bf16[8,64,64,128]{2,1,3,0:T(8,128)(2,1)} %copy.830), kind=kOutput, calls=%fused_computation.603 | convolution fusion | flops 33554432 | bytes 9961472 | tf_op jit(solution)/shard_map/sabp,svbp->svap/dot_general | solution.py:40
  672.5 5.3 fusion.427
  678.5 12.2 %fusion.437 = f32[8,128,4,64]{3,2,1,0:T(4,128)S(1)} fusion(bf16[8,4,64,128]{2,1,3,0:T(4,128)(2,1)S(1)} %copy.990, bf16[8,64,64,128]{2,1,3,0:T(8,128)(2,1)} %copy.823), kind=kOutput, calls=%fused_computation.604 | convolution fusion | flops 33554432 | bytes 9961472 | tf_op jit(solution)/shard_map/sabp,svbp->svap/dot_general | solution.py:40
  (484 shorter events, 354.9 us)
Async XLA Ops:
  41.1 10.9 %collective-permute-start = (bf16[2,4,64,128]{3,2,1,0:T(8,128)(2,1)S(1)}, bf16[2,4,64,128]{3,2,1,0:T(8,128)(2,1)S(1)}, u32[]{:S(2)}, u32[]{:S(2)}) collective-permute-start(bf16[2,4,64,128]{3,2,1,0:T(8,128)(2,1)S(1)} %get-tuple-element.43), channel_id=1, source_target_pairs={{0,4},{4,8},{8,12},{12,16},{16,20},{20,24},{24,28},{28,32},{32,36}... | collective-permute-start | bytes 393224 | tf_op jit(solution)/shard_map/ppermute | solution.py:26
  41.2 10.8 %collective-permute-start.1 = (bf16[2,4,64,128]{3,2,1,0:T(8,128)(2,1)S(1)}, bf16[2,4,64,128]{3,2,1,0:T(8,128)(2,1)S(1)}, u32[]{:S(2)}, u32[]{:S(2)}) collective-permute-start(bf16[2,4,64,128]{3,2,1,0:T(8,128)(2,1)S(1)} %get-tuple-element.44), channel_id=1, source_target_pairs={{4,0},{8,4},{12,8},{16,12},{20,16},{24,20},{28,24},{32,28},{36,32}... | collective-permute-start | bytes 393224 | tf_op jit(solution)/shard_map/ppermute | solution.py:28
  54.7 30.3 %collective-permute-start.2 = (bf16[12,4,64,2]{2,1,3,0:T(4,128)(2,1)}, bf16[12,4,64,2]{2,1,3,0:T(4,128)(2,1)}, u32[]{:S(2)}, u32[]{:S(2)}) collective-permute-start(bf16[12,4,64,2]{2,1,3,0:T(4,128)(2,1)} %copy.825), channel_id=1, source_target_pairs={{0,1},{1,2},{2,3},{3,0},{4,5},{5,6},{6,7},{7,4},{8,9},{9,10},{10,1... | collective-permute-start | bytes 36872 | tf_op jit(solution)/shard_map/ppermute | solution.py:26
  57.2 29.9 %collective-permute-start.3 = (bf16[12,4,64,2]{2,1,3,0:T(4,128)(2,1)}, bf16[12,4,64,2]{2,1,3,0:T(4,128)(2,1)}, u32[]{:S(2)}, u32[]{:S(2)}) collective-permute-start(bf16[12,4,64,2]{2,1,3,0:T(4,128)(2,1)} %copy.826), channel_id=1, source_target_pairs={{1,0},{2,1},{3,2},{0,3},{5,4},{6,5},{7,6},{4,7},{9,8},{10,9},{11,1... | collective-permute-start | bytes 36872 | tf_op jit(solution)/shard_map/ppermute | solution.py:28
  143.1 7.8 %collective-permute-start.4 = (bf16[2,4,64,128]{3,2,1,0:T(8,128)(2,1)S(1)}, bf16[2,4,64,128]{3,2,1,0:T(8,128)(2,1)S(1)}, u32[]{:S(2)}, u32[]{:S(2)}) collective-permute-start(bf16[2,4,64,128]{3,2,1,0:T(8,128)(2,1)S(1)} %get-tuple-element.41), channel_id=1, source_target_pairs={{0,4},{4,8},{8,12},{12,16},{16,20},{20,24},{24,28},{28,32},{32,36}... | collective-permute-start | bytes 393224 | tf_op jit(solution)/shard_map/ppermute | solution.py:26
  143.2 7.7 %collective-permute-start.5 = (bf16[2,4,64,128]{3,2,1,0:T(8,128)(2,1)S(1)}, bf16[2,4,64,128]{3,2,1,0:T(8,128)(2,1)S(1)}, u32[]{:S(2)}, u32[]{:S(2)}) collective-permute-start(bf16[2,4,64,128]{3,2,1,0:T(8,128)(2,1)S(1)} %get-tuple-element.42), channel_id=1, source_target_pairs={{4,0},{8,4},{12,8},{16,12},{20,16},{24,20},{28,24},{32,28},{36,32}... | collective-permute-start | bytes 393224 | tf_op jit(solution)/shard_map/ppermute | solution.py:28
  153.6 71.4 %collective-permute-start.6 = (bf16[12,4,64,2]{2,1,3,0:T(4,128)(2,1)}, bf16[12,4,64,2]{2,1,3,0:T(4,128)(2,1)S(1)}, u32[]{:S(2)}, u32[]{:S(2)}) collective-permute-start(bf16[12,4,64,2]{2,1,3,0:T(4,128)(2,1)} %copy.835), channel_id=1, source_target_pairs={{0,1},{1,2},{2,3},{3,0},{4,5},{5,6},{6,7},{7,4},{8,9},{9,10},{10,1... | collective-permute-start | bytes 36872 | tf_op jit(solution)/shard_map/ppermute | solution.py:26
  154.3 72.0 %collective-permute-start.7 = (bf16[12,4,64,2]{2,1,3,0:T(4,128)(2,1)S(1)}, bf16[12,4,64,2]{2,1,3,0:T(4,128)(2,1)S(1)}, u32[]{:S(2)}, u32[]{:S(2)}) collective-permute-start(bf16[12,4,64,2]{2,1,3,0:T(4,128)(2,1)S(1)} %copy.836), channel_id=1, source_target_pairs={{1,0},{2,1},{3,2},{0,3},{5,4},{6,5},{7,6},{4,7},{9,8},{10,9},{11,1... | collective-permute-start | bytes 36872 | tf_op jit(solution)/shard_map/ppermute | solution.py:28
  262.9 10.9 %collective-permute-start.8 = (f32[1,1,32,256]{3,2,1,0:T(8,128)S(1)}, f32[1,1,32,256]{3,2,1,0:T(8,128)S(1)}, u32[]{:S(2)}, u32[]{:S(2)}) collective-permute-start(f32[1,1,32,256]{3,2,1,0:T(8,128)S(1)} %div.158), channel_id=1, source_target_pairs={{0,4},{4,8},{8,12},{12,16},{16,20},{20,24},{24,28},{28,32},{32,36}... | collective-permute-start | bytes 98312 | tf_op jit(solution)/shard_map/ppermute | solution.py:26
  268.7 6.7 collective-permute-start.9
  298.8 6.7 collective-permute-start.12
  298.9 6.7 collective-permute-start.13
  305.6 5.9 collective-permute-start.14
  328.1 6.7 collective-permute-start.16
  328.1 6.7 collective-permute-start.17
  334.8 6.0 collective-permute-start.18
  357.8 6.7 collective-permute-start.20
  357.9 6.7 collective-permute-start.21
  364.6 5.9 collective-permute-start.22
  387.5 6.7 collective-permute-start.24
  387.6 6.7 collective-permute-start.25
  417.6 6.7 collective-permute-start.28
  417.7 6.7 collective-permute-start.29
  447.4 6.7 collective-permute-start.32
  447.5 6.7 collective-permute-start.33
  478.6 7.8 %collective-permute-start.36 = (bf16[2,4,64,128]{3,2,1,0:T(8,128)(2,1)S(1)}, bf16[2,4,64,128]{3,2,1,0:T(8,128)(2,1)S(1)}, u32[]{:S(2)}, u32[]{:S(2)}) collective-permute-start(bf16[2,4,64,128]{3,2,1,0:T(8,128)(2,1)S(1)} %get-tuple-element.39), channel_id=1, source_target_pairs={{0,4},{4,8},{8,12},{12,16},{16,20},{20,24},{24,28},{28,32},{32,36}... | collective-permute-start | bytes 393224 | tf_op jit(solution)/shard_map/ppermute | solution.py:26
  478.7 7.7 %collective-permute-start.37 = (bf16[2,4,64,128]{3,2,1,0:T(8,128)(2,1)S(1)}, bf16[2,4,64,128]{3,2,1,0:T(8,128)(2,1)S(1)}, u32[]{:S(2)}, u32[]{:S(2)}) collective-permute-start(bf16[2,4,64,128]{3,2,1,0:T(8,128)(2,1)S(1)} %get-tuple-element.40), channel_id=1, source_target_pairs={{4,0},{8,4},{12,8},{16,12},{20,16},{24,20},{28,24},{32,28},{36,32}... | collective-permute-start | bytes 393224 | tf_op jit(solution)/shard_map/ppermute | solution.py:28
  551.0 7.8 %collective-permute-start.40 = (bf16[2,4,64,128]{3,2,1,0:T(8,128)(2,1)S(1)}, bf16[2,4,64,128]{3,2,1,0:T(8,128)(2,1)S(1)}, u32[]{:S(2)}, u32[]{:S(2)}) collective-permute-start(bf16[2,4,64,128]{3,2,1,0:T(8,128)(2,1)S(1)} %get-tuple-element.37), channel_id=1, source_target_pairs={{0,4},{4,8},{8,12},{12,16},{16,20},{20,24},{24,28},{28,32},{32,36}... | collective-permute-start | bytes 393224 | tf_op jit(solution)/shard_map/ppermute | solution.py:26
  551.1 7.7 %collective-permute-start.41 = (bf16[2,4,64,128]{3,2,1,0:T(8,128)(2,1)S(1)}, bf16[2,4,64,128]{3,2,1,0:T(8,128)(2,1)S(1)}, u32[]{:S(2)}, u32[]{:S(2)}) collective-permute-start(bf16[2,4,64,128]{3,2,1,0:T(8,128)(2,1)S(1)} %get-tuple-element.38), channel_id=1, source_target_pairs={{4,0},{8,4},{12,8},{16,12},{20,16},{24,20},{28,24},{32,28},{36,32}... | collective-permute-start | bytes 393224 | tf_op jit(solution)/shard_map/ppermute | solution.py:28
  623.9 7.8 %collective-permute-start.44 = (bf16[2,4,64,128]{3,2,1,0:T(8,128)(2,1)S(1)}, bf16[2,4,64,128]{3,2,1,0:T(8,128)(2,1)S(1)}, u32[]{:S(2)}, u32[]{:S(2)}) collective-permute-start(bf16[2,4,64,128]{3,2,1,0:T(8,128)(2,1)S(1)} %get-tuple-element.35), channel_id=1, source_target_pairs={{0,4},{4,8},{8,12},{12,16},{16,20},{20,24},{24,28},{28,32},{32,36}... | collective-permute-start | bytes 393224 | tf_op jit(solution)/shard_map/ppermute | solution.py:26
  624.0 7.7 %collective-permute-start.45 = (bf16[2,4,64,128]{3,2,1,0:T(8,128)(2,1)S(1)}, bf16[2,4,64,128]{3,2,1,0:T(8,128)(2,1)S(1)}, u32[]{:S(2)}, u32[]{:S(2)}) collective-permute-start(bf16[2,4,64,128]{3,2,1,0:T(8,128)(2,1)S(1)} %get-tuple-element.36), channel_id=1, source_target_pairs={{4,0},{8,4},{12,8},{16,12},{20,16},{24,20},{28,24},{32,28},{36,32}... | collective-permute-start | bytes 393224 | tf_op jit(solution)/shard_map/ppermute | solution.py:28
  635.0 5.9 collective-permute-start.47
  (74 other events, 585.0 us)
where the time goes:
time: 704 us; the launch traced here: 695 us
  matrix products  314 us (45%)
  local copies, waits for them, and re-layouts  129 us (18%)
  starting transfers between devices  105 us (15%)
  blocking collectives  63.8 us (9%)
  waiting for transfers between devices  44.1 us (6%)
  other arithmetic  36.5 us (5%)
    dot_general x10, matrix products, block_product(): jnp.einsum('sabp,svbp->svap', blocks, operand, preferred_element_type=jnp...  129 us
    dot_general x35, matrix products, coarse_apply(): jnp.einsum('qgab,qgvb->qgva', blocks[:, :, number], picked, precision=PRE...  103 us
    ppermute x24, starting transfers between devices, padded_2(): lax.ppermute(head, axis, [((i + 1) % count, i) for i in range(count)])  89 us
    dot_general x40, matrix products, apply_padded(): jnp.einsum('ab,svbp->svap', couplings[number], shifted, preferred_element...  73.9 us
    pmax x1, blocking collectives, local(): lax.pmax(row_bound(own_blocks, own_shift, own_live, coarse_speed), ('stre...  63.8 us
    unnamed x121, local copies, waits for them, and re-layouts  57 us
    ppermute x24, waiting for transfers between devices, padded_2(): lax.ppermute(tail, axis, [(i, (i + 1) % count) for i in range(count)])  38.9 us
    dot_general x10, local copies, waits for them, and re-layouts, block_product(): jnp.einsum('sabp,svbp->svap', blocks, operand, preferred_element_type=jnp...  21.6 us
  transfers between devices with their start and end apart: 48, of which 27 were waited for; matrix products, arithmetic and copies ran while one was open for 7% of the time, Pallas kernels for 0%

commit v1 on v0

v1 whole, which is shorter than its diff:
```python
import functools

import jax
import jax.numpy as jnp
from jax import lax
from jax.experimental import pallas as pl
from jax.experimental.pallas import tpu as pltpu
from jax.sharding import PartitionSpec as P

OMEGA = 0.3
CHEB = 8
BF = jnp.bfloat16
F32 = jnp.float32
MESH = pl.DeviceIdType.MESH
NT = (((1,), (1,)), ((), ()))
PAIRS = 4
ROWS = 512
EDGE = 16
WROWS = ROWS + 2 * EDGE
UNROLL = 16


def iota(shape, dim):
    return lax.broadcasted_iota(jnp.int32, shape, dim)


def one_zero(mask):
    return jnp.where(mask, 1.0, 0.0).astype(BF)


def dot(left, right):
    return jnp.dot(left, right, preferred_element_type=F32)


def dot_nt(left, right):
    return lax.dot_general(left, right, NT, preferred_element_type=F32)


def hi_lo(value):
    high = value.astype(BF)
    return high, (value - high.astype(F32)).astype(BF)


def block_tile(blocks, low, quad, step):
    left_half = iota((16, 128), 1) < 64
    none = jnp.zeros((16, 128), BF)
    first, second = low
    operand = jnp.concatenate(
        [
            jnp.concatenate([jnp.where(left_half, first, none), none], 1),
            jnp.concatenate([jnp.where(left_half, none, first), none], 1),
            jnp.concatenate([none, jnp.where(left_half, second, none)], 1),
            jnp.concatenate([none, jnp.where(left_half, none, second)], 1),
        ],
        0,
    )
    rows = pl.ds(pl.multiple_of(step * 256, 256), 256)
    weights = jnp.concatenate([blocks[2 * quad, rows, :], blocks[2 * quad + 1, rows, :]], 1)
    product = dot_nt(operand, weights)
    top = iota((8, 128), 0) < 4
    left = iota((8, 128), 1) < 64
    results = []
    for half in range(2):
        pieces = []
        for part in range(2):
            even = product[32 * half + 8 * part : 32 * half + 8 * part + 8, 128 * part : 128 * part + 128]
            odd = product[32 * half + 16 + 8 * part : 32 * half + 24 + 8 * part, 128 * part : 128 * part + 128]
            kept = jnp.where(top, even, odd)
            moved = pltpu.roll(jnp.where(top, odd, even), 64, 1)
            pieces.append(jnp.where(top == left, kept, moved))
        results.append(jnp.concatenate(pieces, 0))
    return results


def relayout(raw, blocks, pair):
    def some_rows(group, carry):
        turned = []
        for number in range(16):
            row = group * 16 + number
            source = jnp.concatenate([raw[2 * pair, row], raw[2 * pair + 1, row]], 0)
            turned.append(source.T)
        for part in range(8):
            cube = jnp.stack([one[16 * part : 16 * part + 16] for one in turned], 0)
            cube = jnp.transpose(cube, (1, 0, 2))
            for node in range(16):
                place = pl.multiple_of((part * 16 + node) * 64 + group * 16, 16)
                blocks[pair, pl.ds(place, 16), :] = cube[node]
        return carry

    lax.fori_loop(0, 4, some_rows, 0)


def kernel(
    stream_total,
    span_total,
    rhs_hbm, shift_hbm, diag_hbm, smooth_hbm, couple_hbm, coef_hbm, ids_hbm, cols_hbm, coarse_hbm, cshift_hbm,
    out_hbm,
    raw_rhs, raw_shift, raw_diag, raw_smooth, raw_couple, raw_coef, raw_ids, raw_cols, raw_coarse, raw_cshift,
    diag, smoother, rhs, shift, inverse, field, image, residual, low, wide, coef, couple,
    member, member_t, spread, pick, live, cshift, z_now, t_now, d_now, coarse_own, coarse_got, picked,
    bound, bound_got, idpad,
    load_sem, halo_send, halo_recv, coarse_send, coarse_recv, bound_send, bound_recv, store_sem,
):
    position = lax.axis_index("stream")
    across = lax.axis_index("span")
    after = lax.rem(position + 1, stream_total)
    before = lax.rem(position + stream_total - 1, stream_total)
    right = lax.rem(across + 1, span_total)
    left = lax.rem(across + span_total - 1, span_total)
    group = min(8, stream_total)
    groups = stream_total // group

    stages = [[], [], []]
    for step in range(1, span_total):
        stages[0].append((position, lax.rem(across + step, span_total)))
    base = (position // group) * group
    for step in range(1, group):
        stages[1].append((base + lax.rem(position - base + step, group), across))
    for step in range(1, groups):
        stages[2].append((lax.rem(position + step * group, stream_total), across))
    partners = [who for stage in stages for who in stage]
    greeted = partners + [(after, across), (before, across)]

    barrier = pltpu.get_barrier_semaphore()
    for who in greeted:
        pl.semaphore_signal(barrier, inc=1, device_id=who, device_id_type=MESH)

    loads = []

    def load(source, target):
        copy = pltpu.make_async_copy(source, target, load_sem.at[len(loads)])
        copy.start()
        loads.append(copy)
        return copy

    load_rhs = load(rhs_hbm, raw_rhs)
    load_shift = load(shift_hbm, raw_shift)
    load_ids = load(ids_hbm, raw_ids)
    load_cols = load(cols_hbm, raw_cols)
    load_cshift = load(cshift_hbm, raw_cshift)
    load_couple = load(couple_hbm, raw_couple)
    load_coef = load(coef_hbm, raw_coef)
    load_smooth = [
        load(smooth_hbm.at[pl.ds(2 * pair, 2)], raw_smooth.at[pl.ds(2 * pair, 2)]) for pair in range(PAIRS)
    ]
    load_coarse = load(coarse_hbm, raw_coarse)
    load_diag = [load(diag_hbm.at[pl.ds(2 * pair, 2)], raw_diag.at[pl.ds(2 * pair, 2)]) for pair in range(PAIRS)]

    def speed_of(place, extent):
        return jnp.sqrt(1.0 + 8.0 * (place + 0.5) / extent)

    here = position.astype(F32)
    coarse_speed = speed_of(jnp.full((1, 128), here, F32), float(stream_total))

    def spread_part(number, carry):
        rows = iota((128, 128), 0)
        lanes = iota((128, 128), 1)
        want = 2 * number + lax.shift_right_logical(rows, 6)
        spread[pl.ds(pl.multiple_of(number * 128, 128), 128), :] = one_zero((lanes & 63) == want)
        return carry

    lax.fori_loop(0, 32, spread_part, 0)

    load_rhs.wait()
    for pair in range(PAIRS):
        for vector in range(4):
            block = jnp.concatenate([raw_rhs[2 * pair, vector], raw_rhs[2 * pair + 1, vector]], 0)
            rhs[pair, pl.ds(vector, 128, stride=4), :] = block.T
    load_shift.wait()
    for pair in range(PAIRS):
        block = jnp.concatenate([raw_shift[2 * pair], raw_shift[2 * pair + 1]], 0).T
        for vector in range(4):
            shift[pair, pl.ds(vector, 128, stride=4), :] = block
        block = 1.0 / block
        for vector in range(4):
            inverse[pair, pl.ds(vector, 128, stride=4), :] = block

    load_ids.wait()
    idpad[...] = jnp.zeros(idpad.shape, BF)
    ids16 = jnp.concatenate([raw_ids[...].astype(F32), jnp.zeros((8, 128), F32)], 0).astype(BF)
    idpad[0:16, :] = ids16
    rows = iota((128, 128), 0)
    lanes = iota((128, 128), 1)
    expand = one_zero(lanes == lax.shift_right_logical(rows & 31, 2))
    by_slot = dot(expand, idpad[...])
    slot = (rows & 31).astype(F32)
    found = jnp.max(jnp.where(by_slot == slot, 1.0, 0.0), axis=1, keepdims=True)
    live[...] = jnp.broadcast_to(found, (128, 128))
    by_slot = by_slot.astype(BF)
    rows = iota((128, 512), 0)
    lanes = iota((128, 512), 1)
    node_of = one_zero(lax.shift_right_logical(lanes, 2) == rows)
    wide_ids = dot(by_slot, node_of)
    same = (lanes & 3) == lax.shift_right_logical(rows, 5)
    member[...] = one_zero(jnp.logical_and(wide_ids == (rows & 31).astype(F32), same))
    rows = iota((512, 128), 0)
    lanes = iota((512, 128), 1)
    of_node = one_zero(lax.shift_right_logical(rows, 2) == lanes)
    tall_ids = dot_nt(of_node, by_slot)
    same = (rows & 3) == lax.shift_right_logical(lanes, 5)
    member_t[...] = one_zero(jnp.logical_and(tall_ids == (lanes & 31).astype(F32), same))

    load_cols.wait()
    rows = iota((128, 32), 0)
    lanes = iota((128, 32), 1)
    repeat_rows = (rows & 31) == lanes
    rows = iota((128, 128), 0)
    lanes = iota((128, 128), 1)
    same = lax.shift_right_logical(rows, 5) == lax.shift_right_logical(lanes, 5)
    for number in range(5):
        line = jnp.broadcast_to(raw_cols[number : number + 1, :].astype(F32), (128, 32)).astype(BF)
        column = dot_nt(one_zero(repeat_rows), line)
        chosen = jnp.logical_and(column == (lanes & 31).astype(F32), same)
        if number == 1:
            chosen = jnp.logical_and(chosen, position > 0)
        if number == 2:
            chosen = jnp.logical_and(chosen, position < stream_total - 1)
        pick[number] = one_zero(chosen)

    load_cshift.wait()
    twice = jnp.where((iota((64, 128), 1) & 63) == iota((64, 128), 0), 1.0, 0.0)
    doubled = jnp.dot(raw_cshift[...], twice, precision=lax.Precision.HIGHEST, preferred_element_type=F32)
    for vector in range(4):
        cshift[32 * vector : 32 * vector + 32, :] = doubled

    load_couple.wait()
    for number in range(8):
        one = raw_couple[number].astype(F32)
        none = jnp.zeros((64, 64), F32)
        both = jnp.concatenate([jnp.concatenate([one, none], 1), jnp.concatenate([none, one], 1)], 0)
        couple[number * 128 : number * 128 + 128, :] = both.T.astype(BF)

    load_coef.wait()
    rows = iota((512, 128), 0)
    lanes = iota((512, 128), 1)
    of_node = one_zero(lax.shift_right_logical(rows, 2) == lanes)
    place = iota((8, 128), 0)
    node_speed = speed_of(here * 8.0 + place.astype(F32), float(stream_total * 8))
    first = position == 0
    last = position == stream_total - 1
    for number in range(8):
        weights = node_speed * raw_coef[number]
        if number == 0:
            weights = jnp.where(jnp.logical_and(first, place < 2), 0.0, weights)
        if number == 1:
            weights = jnp.where(jnp.logical_and(first, place < 1), 0.0, weights)
        if number == 2:
            weights = jnp.where(jnp.logical_and(last, place > 6), 0.0, weights)
        if number == 3:
            weights = jnp.where(jnp.logical_and(last, place > 5), 0.0, weights)
        for half in range(2):
            lines = jnp.concatenate(
                [jnp.broadcast_to(weights[4 * half + i : 4 * half + i + 1, :], (64, 128)) for i in range(4)], 0
            ).astype(BF)
            laid = dot_nt(of_node, lines).astype(BF)
            coef[number, 2 * half] = laid[:, :128]
            coef[number, 2 * half + 1] = laid[:, 128:]

    pl.semaphore_wait(barrier, len(greeted))

    bound_copies = [
        pltpu.make_async_remote_copy(
            src_ref=bound.at[stage],
            dst_ref=bound_got.at[slot_number],
            send_sem=bound_send.at[slot_number],
            recv_sem=bound_recv.at[slot_number],
            device_id=who,
            device_id_type=MESH,
        )
        for slot_number, (stage, who) in enumerate(
            [(stage, who) for stage in range(3) for who in stages[stage]]
        )
    ]
    starts = [0, len(stages[0]), len(stages[0]) + len(stages[1]), len(partners)]

    def bound_begin(stage):
        for number in range(starts[stage], starts[stage + 1]):
            bound_copies[number].start()

    def bound_end(stage):
        value = bound[stage]
        for number in range(starts[stage], starts[stage + 1]):
            bound_copies[number].wait()
            value = jnp.maximum(value, bound_got[number])
        bound[stage + 1] = value

    def coarse_bound():
        load_coarse.wait()
        total = jnp.zeros((64, 128), F32)
        for number in range(32):
            columns = slice(128 * number, 128 * number + 128)
            size = jnp.abs(raw_coarse[0, :, columns])
            for kind in range(1, 5):
                size = size + jnp.abs(raw_coarse[kind, :, columns])
            high, rest = hi_lo(size)
            total = total + dot(jnp.concatenate([high, rest], 0), spread[columns, :])
        largest = live[0:32, :] * (cshift[0:32, :] + coarse_speed * (total[0:32] + total[32:64]))
        bound[0] = jnp.broadcast_to(jnp.max(jnp.max(largest, axis=1, keepdims=True), axis=0, keepdims=True), (8, 128))

    def halo_copies(parity):
        def copy(number, source, target, who):
            return pltpu.make_async_remote_copy(
                src_ref=source,
                dst_ref=target,
                send_sem=halo_send.at[parity, number],
                recv_sem=halo_recv.at[parity, number],
                device_id=who,
                device_id_type=MESH,
            )

        mine = pl.ds(EDGE, ROWS)
        inner = pl.ds(1, PAIRS)
        return [
            copy(0, wide.at[parity, PAIRS, mine], wide.at[parity, 0, mine], (after, across)),
            copy(1, wide.at[parity, 1, mine], wide.at[parity, PAIRS + 1, mine], (before, across)),
            copy(2, wide.at[parity, inner, pl.ds(ROWS, EDGE)], wide.at[parity, inner, pl.ds(0, EDGE)], (position, right)),
            copy(3, wide.at[parity, inner, pl.ds(EDGE, EDGE)], wide.at[parity, inner, pl.ds(ROWS + EDGE, EDGE)], (position, left)),
        ]

    def smooth_step(parity):
        following = 1 - parity

        def tiles(number, carry):
            for inside in range(UNROLL):
                tile = number * UNROLL + inside
                quad, step = tile // 32, lax.rem(tile, 32)
                rows = pl.ds(pl.multiple_of(step * 16, 16), 16)
                shifted = pl.ds(pl.multiple_of(step * 16 + EDGE, 16), 16)
                operand = [low[2 * quad + half, rows, :] for half in range(2)]
                parts = block_tile(smoother, operand, quad, step)
                for half in range(2):
                    pair = 2 * quad + half
                    change = residual[pair, rows, :] * inverse[pair, rows, :] + parts[half]
                    value = field[pair, rows, :] + OMEGA * change
                    field[pair, rows, :] = value
                    wide[following, pair + 1, shifted, :] = value.astype(BF)
            return carry

        lax.fori_loop(0, 64 // UNROLL, tiles, 0)

    def operator_inner(parity):
        def tiles(number, carry):
            for inside in range(UNROLL):
                tile = number * UNROLL + inside
                quad, step = tile // 32, lax.rem(tile, 32)
                rows = pl.ds(pl.multiple_of(step * 16, 16), 16)
                shifted = pl.ds(pl.multiple_of(step * 16 + EDGE, 16), 16)
                operand = [wide[parity, 2 * quad + half + 1, shifted, :] for half in range(2)]
                parts = block_tile(diag, operand, quad, step)
                for half in range(2):
                    pair = 2 * quad + half
                    image[pair, rows, :] = shift[pair, rows, :] * operand[half].astype(F32) + parts[half]
            return carry

        lax.fori_loop(0, 64 // UNROLL, tiles, 0)

    def operator_outer(parity, scale):
        left_half = iota((128, 128), 1) < 64

        def chunks(number, carry):
            pair, start = number // 4, lax.rem(number, 4) * 128
            rows = pl.ds(pl.multiple_of(start, 128), 128)

            def at(which):
                return wide[parity, which, pl.ds(pl.multiple_of(start + EDGE, 16), 128), :]

            here_now, lower, upper = at(pair + 1), at(pair), at(pair + 2)
            around = wide[parity, pair + 1, pl.ds(pl.multiple_of(start, 16), 128 + 2 * EDGE), :]
            shifted = [
                lower,
                pltpu.roll(jnp.where(left_half, here_now, lower).astype(F32), 64, 1).astype(BF),
                pltpu.roll(jnp.where(left_half, upper, here_now).astype(F32), 64, 1).astype(BF),
                upper,
                around[EDGE - 8 : EDGE + 120],
                around[EDGE - 4 : EDGE + 124],
                around[EDGE + 4 : EDGE + 132],
                around[EDGE + 8 : EDGE + 136],
            ]
            operand = jnp.concatenate([coef[m, pair, rows, :] * shifted[m] for m in range(8)], 1)
            value = scale * rhs[pair, rows, :] - (image[pair, rows, :] + dot(operand, couple[...]))
            residual[pair, rows, :] = value
            low[pair, rows, :] = value.astype(BF)
            return carry

        lax.fori_loop(0, 16, chunks, 0)

    def coarse_copies(parity):
        targets = [(after, across), (before, across), (position, right), (position, left)]
        return [
            pltpu.make_async_remote_copy(
                src_ref=coarse_own.at[parity],
                dst_ref=coarse_got.at[parity, number],
                send_sem=coarse_send.at[parity, number],
                recv_sem=coarse_recv.at[parity, number],
                device_id=who,
                device_id_type=MESH,
            )
            for number, who in enumerate(targets)
        ]

    def restrict():
        total = jnp.zeros((128, 512), F32)
        parts = []
        for pair in range(PAIRS):
            high, rest = hi_lo(residual[pair])
            parts.append(dot(member[...], high) + dot(member[...], rest))
        left_half = iota((8, 128), 1) < 64
        top = iota((8, 128), 0) < 4
        for vector in range(4):
            for pair in range(PAIRS):
                begin = 32 * vector + 8 * pair
                own = jnp.where(top == left_half, parts[pair][begin : begin + 8, :], 0.0)
                t_now[begin : begin + 8, :] = own + pltpu.roll(own, 64, 1)

    def coarse_product(got):
        for number in range(5):
            value = dot(pick[number], got[number])
            picked[number] = value + pltpu.roll(value, 64, 1)
        total = jnp.zeros((128, 128), F32)
        for column in range(16):
            sides = []
            for side in range(2):
                begin = 256 * column + 128 * side
                blocks = [raw_coarse[k, :, begin : begin + 128] for k in range(5)]
                pieces = []
                for vector in range(4):
                    part = blocks[0] * picked[0, 32 * vector : 32 * vector + 32, :]
                    for k in range(1, 5):
                        part = part + blocks[k] * picked[k, 32 * vector : 32 * vector + 32, :]
                    pieces.append(part.astype(BF))
                sides.append(jnp.concatenate(pieces, 0))
            operand = jnp.concatenate(sides, 1)
            total = total + dot(operand, spread[256 * column : 256 * column + 256, :])
        return total

    def coarse_solve():
        upper_edge = 1.05 * bound[3]
        lower_edge = upper_edge / 20.0
        middle = 0.5 * (upper_edge + lower_edge)
        gap = 0.5 * (upper_edge - lower_edge)
        sigma = middle / gap
        restrict()
        d_now[...] = t_now[...] / middle[0:1, :]
        z_now[...] = jnp.zeros((128, 128), F32)
        left_half = iota((128, 128), 1) < 64

        def step(number, rho):
            parity = lax.rem(number, 2)
            direction = d_now[...]
            high, rest = hi_lo(direction)
            coarse_own[parity] = jnp.where(left_half, high, rest)
            copies = coarse_copies(parity)
            for copy in copies:
                copy.start()
            z_now[...] = z_now[...] + direction
            for copy in copies:
                copy.wait()
            got = [coarse_own[parity]] + [coarse_got[parity, k] for k in range(4)]
            coupled = coarse_product(got)
            t_next = t_now[...] - live[...] * (cshift[...] * direction + coarse_speed * coupled)
            t_now[...] = t_next
            rho_next = 1.0 / (2.0 * sigma - rho)
            d_now[...] = (rho_next * rho)[0:1, :] * direction + (2.0 * rho_next / gap)[0:1, :] * t_next
            return rho_next

        lax.fori_loop(0, CHEB - 1, step, 1.0 / sigma)
        z_now[...] = z_now[...] + d_now[...]

    def prolong(parity):
        following = 1 - parity
        slots = lax.shift_right_logical(iota((128, 128), 0) & 31, 2)
        half = lax.shift_right_logical(iota((128, 128), 1), 6)
        twice = jnp.concatenate([member_t[...], member_t[...]], 1)
        for pair in range(PAIRS):
            high, rest = hi_lo(jnp.where(slots == 2 * pair + half, z_now[...], 0.0))
            value = dot(twice, jnp.concatenate([high, rest], 0))
            field[pair] = field[pair] + value
            wide[following, pair + 1, EDGE : EDGE + ROWS, :] = value.astype(BF)

    field[...] = jnp.zeros(field.shape, F32)
    for pair in range(PAIRS):
        residual[pair] = rhs[pair]
        low[pair] = rhs[pair].astype(BF)

    def round_of(number, carry):
        parity = lax.rem(number, 2)

        @pl.when(number == 0)
        def _():
            for pair in range(PAIRS):
                load_smooth[pair].wait()
                relayout(raw_smooth, smoother, pair)
            coarse_bound()
            bound_begin(0)

        @pl.when(number > 0)
        def _():
            operator_inner(parity)
            copies = halo_copies(parity)
            for copy in copies:
                copy.wait()
            scale = jnp.where(number == 3, 0.0, 1.0)
            operator_outer(parity, scale)

        @pl.when(number == 2)
        def _():
            bound_end(2)
            coarse_solve()
            prolong(parity)

        @pl.when(number != 2)
        def _():
            smooth_step(parity)

        @pl.when(number < 5)
        def _():
            for copy in halo_copies(1 - parity):
                copy.start()

        @pl.when(number == 0)
        def _():
            bound_end(0)
            bound_begin(1)
            for pair in range(PAIRS):
                load_diag[pair].wait()
                relayout(raw_diag, diag, pair)

        @pl.when(number == 1)
        def _():
            bound_end(1)
            bound_begin(2)

        return carry

    lax.fori_loop(0, 6, round_of, 0)

    stores = []
    for pair in range(PAIRS):
        for vector in range(4):
            block = field[pair, pl.ds(vector, 128, stride=4), :].T
            raw_rhs[2 * pair, vector] = block[0:64]
            raw_rhs[2 * pair + 1, vector] = block[64:128]
        copy = pltpu.make_async_copy(
            raw_rhs.at[pl.ds(2 * pair, 2)], out_hbm.at[pl.ds(2 * pair, 2)], store_sem.at[pair]
        )
        copy.start()
        stores.append(copy)
    for copy in stores:
        copy.wait()


def local(stream_total, span_total, right_side, shift_fine, diag_blocks, smoother, couplings, coefficients,
          agg_ids, coarse_columns, coarse_blocks, coarse_shift):
    columns = jnp.transpose(coarse_columns[0, 0], (1, 0))
    blocks = jnp.transpose(coarse_blocks[0, 0], (1, 0, 2))
    vm = pltpu.VMEM
    dma = pltpu.SemaphoreType.DMA
    partners = (span_total - 1) + (min(8, stream_total) - 1) + (stream_total // min(8, stream_total) - 1)
    shape = (PAIRS, ROWS, 128)
    scratch = [
        vm((8, 4, 64, 128), F32), vm((8, 64, 128), F32), vm((8, 64, 64, 128), BF), vm((8, 64, 64, 128), BF),
        vm((8, 64, 64), BF), vm((8, 8, 128), F32), vm((8, 128), jnp.int32), vm((5, 32), jnp.int32),
        vm((5, 32, 4096), F32), vm((32, 64), F32),
        vm((PAIRS, 8192, 128), BF), vm((PAIRS, 8192, 128), BF), vm(shape, F32), vm(shape, F32), vm(shape, F32),
        vm(shape, F32), vm(shape, F32), vm(shape, F32), vm(shape, BF), vm((2, PAIRS + 2, WROWS, 128), BF),
        vm((8,) + shape, BF), vm((1024, 128), BF),
        vm((128, 512), BF), vm((512, 128), BF), vm((4096, 128), BF), vm((5, 128, 128), BF), vm((128, 128), F32),
        vm((128, 128), F32), vm((128, 128), F32), vm((128, 128), F32), vm((128, 128), F32),
        vm((2, 128, 128), BF), vm((2, 4, 128, 128), BF), vm((5, 128, 128), F32),
        vm((4, 8, 128), F32), vm((partners, 8, 128), F32), vm((128, 128), BF),
        dma((16,)), dma((2, 4)), dma((2, 4)), dma((2, 4)), dma((2, 4)), dma((partners,)), dma((partners,)), dma((4,)),
    ]
    anywhere = pl.BlockSpec(memory_space=pl.ANY)
    return pl.pallas_call(
        functools.partial(kernel, stream_total, span_total),
        out_shape=jax.ShapeDtypeStruct(right_side.shape, F32),
        in_specs=[anywhere] * 10,
        out_specs=anywhere,
        scratch_shapes=scratch,
        compiler_params=pltpu.CompilerParams(
            collective_id=0, has_side_effects=True, vmem_limit_bytes=60 * 1024 * 1024
        ),
        name="cycle",
    )(right_side, shift_fine, diag_blocks, smoother, couplings, coefficients, agg_ids, columns, blocks,
      coarse_shift[0, 0])


def solution(mesh):
    return jax.shard_map(
        functools.partial(local, mesh.shape["stream"], mesh.shape["span"]),
        mesh=mesh,
        in_specs=(
            P("stream", None, None, "span"),
            P("stream", None, "span"),
            P("stream", None, None, "span"),
            P("stream", None, None, "span"),
            P(),
            P(None, "stream", "span"),
            P("stream", "span"),
            P("stream", "span", None, None),
            P("stream", "span", None, None, None),
            P("stream", "span", None, None),
        ),
        out_specs=P("stream", None, None, "span"),
        check_vma=False,
    )
```

time: 704 us -> 128 us (0.18); the launches traced: 695 us -> 127 us
  matrix products: 314 us -> 0 us
  local copies, waits for them, and re-layouts: 129 us -> 3.58 us
  Pallas kernels: 0 us -> 124 us
  starting transfers between devices: 105 us -> 0 us
  blocking collectives: 63.8 us -> 0 us
  waiting for transfers between devices: 44.1 us -> 0 us
  other arithmetic: 36.5 us -> 0 us
    dot_general x122 -> x0, matrix products: 314 us -> none  [the longest x10 129 us: block_product(): jnp.einsum('sabp,svbp->svap', blocks, operand, preferred_element_type=jnp...]
    pallas_call x0 -> x1, Pallas kernels: none -> 124 us  [local(): pl.pallas_call(functools.partial(kernel, stream_total, span_total), out_s...]
    ppermute x48 -> x0, starting transfers between devices: 105 us -> none  [the longest x24 89 us: padded_2(): lax.ppermute(head, axis, [((i + 1) % count, i) for i in range(count)])]
    pmax x1 -> x0, blocking collectives: 63.8 us -> none  [local(): lax.pmax(row_bound(own_blocks, own_shift, own_live, coarse_speed), ('stre...]
    unnamed x121 -> x2, local copies, waits for them, and re-layouts: 57 us -> 3.58 us
    ppermute x48 -> x0, waiting for transfers between devices: 44.1 us -> none  [the longest x24 38.9 us: padded_2(): lax.ppermute(tail, axis, [(i, (i + 1) % count) for i in range(count)])]
    dot_general x52 -> x0, local copies, waits for them, and re-layouts: 25.3 us -> none  [the longest x10 21.6 us: block_product(): jnp.einsum('sabp,svbp->svap', blocks, operand, preferred_element_type=jnp...]
    slice x30 -> x0, local copies, waits for them, and re-layouts: 17.3 us -> none  [the longest x10 8.08 us: apply_padded(): center = padded[2:stream_count + 2, :, :, 2:span_count + 2]]
  transfers between devices with their start and end apart: 48 -> 0, of which waited for: 27 -> 0; matrix products, arithmetic and copies ran while one was open for 7% -> 0% of each run, Pallas kernels for 0% -> 0%
where the time goes in v1:
time: 128 us; the launch traced here: 127 us
  Pallas kernels  124 us (97%)
  local copies, waits for them, and re-layouts  3.58 us (3%)
    pallas_call x1, Pallas kernels, local(): pl.pallas_call(functools.partial(kernel, stream_total, span_total), out_s...  124 us
    unnamed x2, local copies, waits for them, and re-layouts  3.58 us

profile of v1, /device:TPU:0, one launch (start us, length us, event | category | flops | bytes accessed | tf_op | source)
XLA Modules:
  0.0 127.4 jit_solution(11466172904318237864)
XLA Ops:
  0.0 1.3 %copy.13 = s32[1,1,32,5]{2,3,1,0:T(8,128)} copy(s32[1,1,32,5]{2,1,3,0:T(1,128)} %param.17) | data formatting | bytes 1280
  1.3 123.8 %cycle.1 = f32[8,4,64,128]{3,2,1,0:T(8,128)} custom-call(f32[8,4,64,128]{3,2,1,0:T(8,128)} %rhs_hbm.1, f32[8,64,128]{2,1,0:T(8,128)} %shift_hbm.1, bf16[8,64,64,128]{3,2,1,0:T(8,128)(2,1)} %diag_hbm.1, bf16[8,64,64,128]{3,2,1,0:T(8,128)(2,1)} %smooth_hbm.1, bf16[8,64,64]{2,1,0:T(8,128)(2,1)} %couple_hbm.1, f32[8,8,128]{2,1,0:T(8,128)} %coef_hbm.1, ...), custom_call_target="tpu_custom_call" | custom-call | tf_op jit(solution)/shard_map/cycle/pallas_call | solution.py:574
  125.1 2.3 %copy.15 = f32[8,4,64,128]{3,2,1,0:T(8,128)} copy(f32[8,4,64,128]{3,2,1,0:T(8,128)} %cycle.1) | data formatting | bytes 2097152

commit v2 on v1

--- a/solution.py
+++ b/solution.py
@@ -17,7 +17,6 @@
 ROWS = 512
 EDGE = 16
 WROWS = ROWS + 2 * EDGE
-UNROLL = 16
 
 
 def iota(shape, dim):
@@ -42,43 +41,39 @@
 
 
 def block_tile(blocks, low, quad, step):
-    left_half = iota((16, 128), 1) < 64
+    left = iota((16, 128), 1) < 64
+    node = lax.shift_right_logical(iota((16, 128), 0), 2)
     none = jnp.zeros((16, 128), BF)
-    first, second = low
-    operand = jnp.concatenate(
-        [
-            jnp.concatenate([jnp.where(left_half, first, none), none], 1),
-            jnp.concatenate([jnp.where(left_half, none, first), none], 1),
-            jnp.concatenate([none, jnp.where(left_half, second, none)], 1),
-            jnp.concatenate([none, jnp.where(left_half, none, second)], 1),
-        ],
-        0,
-    )
+    lines = []
+    for value in low:
+        other = pltpu.roll(value.astype(F32), 64, 1).astype(BF)
+        for even, odd in ((value, other), (other, value)):
+            halves = []
+            for part in range(2):
+                is_even = jnp.logical_and(node == 2 * part, left)
+                is_odd = jnp.logical_and(node == 2 * part + 1, jnp.logical_not(left))
+                halves.append(jnp.where(is_even, even, jnp.where(is_odd, odd, none)))
+            lines.append(jnp.concatenate(halves, 1))
     rows = pl.ds(pl.multiple_of(step * 256, 256), 256)
     weights = jnp.concatenate([blocks[2 * quad, rows, :], blocks[2 * quad + 1, rows, :]], 1)
-    product = dot_nt(operand, weights)
-    top = iota((8, 128), 0) < 4
-    left = iota((8, 128), 1) < 64
+    product = dot(jnp.concatenate(lines, 0), weights)
     results = []
     for half in range(2):
-        pieces = []
-        for part in range(2):
-            even = product[32 * half + 8 * part : 32 * half + 8 * part + 8, 128 * part : 128 * part + 128]
-            odd = product[32 * half + 16 + 8 * part : 32 * half + 24 + 8 * part, 128 * part : 128 * part + 128]
-            kept = jnp.where(top, even, odd)
-            moved = pltpu.roll(jnp.where(top, odd, even), 64, 1)
-            pieces.append(jnp.where(top == left, kept, moved))
-        results.append(jnp.concatenate(pieces, 0))
+        columns = slice(128 * half, 128 * half + 128)
+        first, second = product[32 * half : 32 * half + 16, columns], product[32 * half + 16 : 32 * half + 32, columns]
+        results.append(jnp.where(left, first, second))
     return results
 
 
 def relayout(raw, blocks, pair):
-    def some_rows(group, carry):
-        turned = []
-        for number in range(16):
-            row = group * 16 + number
-            source = jnp.concatenate([raw[2 * pair, row], raw[2 * pair + 1, row]], 0)
-            turned.append(source.T)
+    def some_columns(group, carry):
+        columns = pl.ds(pl.multiple_of(group * 16, 16), 16)
+        cubes = []
+        for half in range(2):
+            for part in range(4):
+                cube = jnp.stack([raw[2 * pair + half, 16 * part + a, columns, :] for a in range(16)], 0)
+                cubes.append(jnp.transpose(cube, (1, 0, 2)))
+        turned = [jnp.concatenate([cube[b] for cube in cubes], 0).T for b in range(16)]
         for part in range(8):
             cube = jnp.stack([one[16 * part : 16 * part + 16] for one in turned], 0)
             cube = jnp.transpose(cube, (1, 0, 2))
@@ -87,7 +82,7 @@
                 blocks[pair, pl.ds(place, 16), :] = cube[node]
         return carry
 
-    lax.fori_loop(0, 4, some_rows, 0)
+    lax.fori_loop(0, 4, some_columns, 0)
 
 
 def kernel(
@@ -97,7 +92,7 @@
     out_hbm,
     raw_rhs, raw_shift, raw_diag, raw_smooth, raw_couple, raw_coef, raw_ids, raw_cols, raw_coarse, raw_cshift,
     diag, smoother, rhs, shift, inverse, field, image, residual, low, wide, coef, couple,
-    member, member_t, spread, pick, live, cshift, z_now, t_now, d_now, coarse_own, coarse_got, picked,
+    member, member_t, spread, pick, live, cshift, z_now, t_now, d_now, coarse_own, coarse_got,
     bound, bound_got, idpad,
     load_sem, halo_send, halo_recv, coarse_send, coarse_recv, bound_send, bound_recv, store_sem,
 ):
@@ -120,6 +115,18 @@
         stages[2].append((lax.rem(position + step * group, stream_total), across))
     partners = [who for stage in stages for who in stage]
     greeted = partners + [(after, across), (before, across)]
+
+    @pl.when(position == 0)
+    def _():
+        for parity in range(2):
+            wide[parity, 0] = jnp.zeros((WROWS, 128), BF)
+            coarse_got[parity, 0] = jnp.zeros((128, 128), BF)
+
+    @pl.when(position == stream_total - 1)
+    def _():
+        for parity in range(2):
+            wide[parity, PAIRS + 1] = jnp.zeros((WROWS, 128), BF)
+            coarse_got[parity, 1] = jnp.zeros((128, 128), BF)
 
     barrier = pltpu.get_barrier_semaphore()
     for who in greeted:
@@ -201,21 +208,16 @@
     member_t[...] = one_zero(jnp.logical_and(tall_ids == (lanes & 31).astype(F32), same))
 
     load_cols.wait()
-    rows = iota((128, 32), 0)
-    lanes = iota((128, 32), 1)
-    repeat_rows = (rows & 31) == lanes
-    rows = iota((128, 128), 0)
-    lanes = iota((128, 128), 1)
+    rows = iota((64, 32), 0)
+    lanes = iota((64, 32), 1)
+    repeat_rows = one_zero((rows & 31) == lanes)
+    rows = iota((64, 64), 0)
+    lanes = iota((64, 64), 1)
     same = lax.shift_right_logical(rows, 5) == lax.shift_right_logical(lanes, 5)
     for number in range(5):
-        line = jnp.broadcast_to(raw_cols[number : number + 1, :].astype(F32), (128, 32)).astype(BF)
-        column = dot_nt(one_zero(repeat_rows), line)
-        chosen = jnp.logical_and(column == (lanes & 31).astype(F32), same)
-        if number == 1:
-            chosen = jnp.logical_and(chosen, position > 0)
-        if number == 2:
-            chosen = jnp.logical_and(chosen, position < stream_total - 1)
-        pick[number] = one_zero(chosen)
+        line = jnp.broadcast_to(raw_cols[number].astype(F32), (64, 32)).astype(BF)
+        column = dot_nt(repeat_rows, line)
+        pick[number] = one_zero(jnp.logical_and(column == (lanes & 31).astype(F32), same))
 
     load_cshift.wait()
     twice = jnp.where((iota((64, 128), 1) & 63) == iota((64, 128), 0), 1.0, 0.0)
@@ -236,18 +238,8 @@
     of_node = one_zero(lax.shift_right_logical(rows, 2) == lanes)
     place = iota((8, 128), 0)
     node_speed = speed_of(here * 8.0 + place.astype(F32), float(stream_total * 8))
-    first = position == 0
-    last = position == stream_total - 1
     for number in range(8):
         weights = node_speed * raw_coef[number]
-        if number == 0:
-            weights = jnp.where(jnp.logical_and(first, place < 2), 0.0, weights)
-        if number == 1:
-            weights = jnp.where(jnp.logical_and(first, place < 1), 0.0, weights)
-        if number == 2:
-            weights = jnp.where(jnp.logical_and(last, place > 6), 0.0, weights)
-        if number == 3:
-            weights = jnp.where(jnp.logical_and(last, place > 5), 0.0, weights)
         for half in range(2):
             lines = jnp.concatenate(
                 [jnp.broadcast_to(weights[4 * half + i : 4 * half + i + 1, :], (64, 128)) for i in range(4)], 0
@@ -297,33 +289,52 @@
         largest = live[0:32, :] * (cshift[0:32, :] + coarse_speed * (total[0:32] + total[32:64]))
         bound[0] = jnp.broadcast_to(jnp.max(jnp.max(largest, axis=1, keepdims=True), axis=0, keepdims=True), (8, 128))
 
-    def halo_copies(parity):
+    def begin(copies):
+        for copy in copies[2:]:
+            copy.start()
+        pl.when(position < stream_total - 1)(copies[0].start)
+        pl.when(position > 0)(copies[1].start)
+
+    def arrived(copies):
+        for copy in copies[2:]:
+            copy.wait_recv()
+        pl.when(position < stream_total - 1)(copies[1].wait_recv)
+        pl.when(position > 0)(copies[0].wait_recv)
+
+    def departed(copies):
+        for copy in copies[2:]:
+            copy.wait_send()
+        pl.when(position < stream_total - 1)(copies[0].wait_send)
+        pl.when(position > 0)(copies[1].wait_send)
+
+    def halo_copies(parity, half):
         def copy(number, source, target, who):
             return pltpu.make_async_remote_copy(
                 src_ref=source,
                 dst_ref=target,
-                send_sem=halo_send.at[parity, number],
-                recv_sem=halo_recv.at[parity, number],
+                send_sem=halo_send.at[parity, half, number],
+                recv_sem=halo_recv.at[parity, half, number],
                 device_id=who,
                 device_id_type=MESH,
             )
 
-        mine = pl.ds(EDGE, ROWS)
+        mine = pl.ds(pl.multiple_of(EDGE + half * (ROWS // 2), 16), ROWS // 2)
         inner = pl.ds(1, PAIRS)
+        edge = pl.ds(pl.multiple_of(EDGE + half * (ROWS - EDGE), 16), EDGE)
+        beyond = pl.ds(pl.multiple_of((1 - half) * (ROWS + EDGE), 16), EDGE)
+        beside = lax.rem(across + span_total - 1 + 2 * half, span_total)
         return [
             copy(0, wide.at[parity, PAIRS, mine], wide.at[parity, 0, mine], (after, across)),
             copy(1, wide.at[parity, 1, mine], wide.at[parity, PAIRS + 1, mine], (before, across)),
-            copy(2, wide.at[parity, inner, pl.ds(ROWS, EDGE)], wide.at[parity, inner, pl.ds(0, EDGE)], (position, right)),
-            copy(3, wide.at[parity, inner, pl.ds(EDGE, EDGE)], wide.at[parity, inner, pl.ds(ROWS + EDGE, EDGE)], (position, left)),
+            copy(2, wide.at[parity, inner, edge], wide.at[parity, inner, beyond], (position, beside)),
         ]
 
-    def smooth_step(parity):
+    def smooth_step(parity, more):
         following = 1 - parity
 
-        def tiles(number, carry):
-            for inside in range(UNROLL):
-                tile = number * UNROLL + inside
-                quad, step = tile // 32, lax.rem(tile, 32)
+        def tiles(part, carry):
+            for inside in range(32):
+                quad, step = inside % 2, part * 16 + inside // 2
                 rows = pl.ds(pl.multiple_of(step * 16, 16), 16)
                 shifted = pl.ds(pl.multiple_of(step * 16 + EDGE, 16), 16)
                 operand = [low[2 * quad + half, rows, :] for half in range(2)]
@@ -334,15 +345,19 @@
                     value = field[pair, rows, :] + OMEGA * change
                     field[pair, rows, :] = value
                     wide[following, pair + 1, shifted, :] = value.astype(BF)
+
+            @pl.when(more)
+            def _():
+                begin(halo_copies(following, part))
+
             return carry
 
-        lax.fori_loop(0, 64 // UNROLL, tiles, 0)
+        lax.fori_loop(0, 2, tiles, 0)
 
     def operator_inner(parity):
-        def tiles(number, carry):
-            for inside in range(UNROLL):
-                tile = number * UNROLL + inside
-                quad, step = tile // 32, lax.rem(tile, 32)
+        def tiles(part, carry):
+            for inside in range(32):
+                quad, step = inside % 2, part * 16 + inside // 2
                 rows = pl.ds(pl.multiple_of(step * 16, 16), 16)
                 shifted = pl.ds(pl.multiple_of(step * 16 + EDGE, 16), 16)
                 operand = [wide[parity, 2 * quad + half + 1, shifted, :] for half in range(2)]
@@ -352,13 +367,12 @@
                     image[pair, rows, :] = shift[pair, rows, :] * operand[half].astype(F32) + parts[half]
             return carry
 
-        lax.fori_loop(0, 64 // UNROLL, tiles, 0)
+        lax.fori_loop(0, 2, tiles, 0)
 
     def operator_outer(parity, scale):
         left_half = iota((128, 128), 1) < 64
 
-        def chunks(number, carry):
-            pair, start = number // 4, lax.rem(number, 4) * 128
+        def chunk(pair, start):
             rows = pl.ds(pl.multiple_of(start, 128), 128)
 
             def at(which):
@@ -380,18 +394,31 @@
             value = scale * rhs[pair, rows, :] - (image[pair, rows, :] + dot(operand, couple[...]))
             residual[pair, rows, :] = value
             low[pair, rows, :] = value.astype(BF)
+
+        for pair in (1, 2):
+            for start in (128, 256):
+                chunk(pair, start)
+        for half in range(2):
+            arrived(halo_copies(parity, half))
+
+        def chunks(number, carry):
+            mixed = number // 2
+            for inside in range(4):
+                pair = mixed * (1 + inside // 2) + (1 - mixed) * 3 * number
+                chunk(pair, 128 * (mixed * 3 * (inside % 2) + (1 - mixed) * inside))
             return carry
 
-        lax.fori_loop(0, 16, chunks, 0)
-
-    def coarse_copies(parity):
+        lax.fori_loop(0, 3, chunks, 0)
+
+    def coarse_copies(parity, half):
         targets = [(after, across), (before, across), (position, right), (position, left)]
+        rows = pl.ds(64 * half, 64)
         return [
             pltpu.make_async_remote_copy(
-                src_ref=coarse_own.at[parity],
-                dst_ref=coarse_got.at[parity, number],
-                send_sem=coarse_send.at[parity, number],
-                recv_sem=coarse_recv.at[parity, number],
+                src_ref=coarse_own.at[parity, rows],
+                dst_ref=coarse_got.at[parity, number, rows],
+                send_sem=coarse_send.at[parity, half, number],
+                recv_sem=coarse_recv.at[parity, half, number],
                 device_id=who,
                 device_id_type=MESH,
             )
@@ -413,24 +440,25 @@
                 t_now[begin : begin + 8, :] = own + pltpu.roll(own, 64, 1)
 
     def coarse_product(got):
+        near = []
         for number in range(5):
             value = dot(pick[number], got[number])
-            picked[number] = value + pltpu.roll(value, 64, 1)
-        total = jnp.zeros((128, 128), F32)
+            near.append(value + pltpu.roll(value, 64, 1))
+        total = jnp.zeros((64, 128), F32)
         for column in range(16):
             sides = []
             for side in range(2):
-                begin = 256 * column + 128 * side
-                blocks = [raw_coarse[k, :, begin : begin + 128] for k in range(5)]
+                begin_at = 256 * column + 128 * side
+                blocks = [raw_coarse[k, :, begin_at : begin_at + 128] for k in range(5)]
                 pieces = []
-                for vector in range(4):
-                    part = blocks[0] * picked[0, 32 * vector : 32 * vector + 32, :]
+                for vector in range(2):
+                    rows = slice(32 * vector, 32 * vector + 32)
+                    part = blocks[0] * near[0][rows]
                     for k in range(1, 5):
-                        part = part + blocks[k] * picked[k, 32 * vector : 32 * vector + 32, :]
+                        part = part + blocks[k] * near[k][rows]
                     pieces.append(part.astype(BF))
                 sides.append(jnp.concatenate(pieces, 0))
-            operand = jnp.concatenate(sides, 1)
-            total = total + dot(operand, spread[256 * column : 256 * column + 256, :])
+            total = total + dot(jnp.concatenate(sides, 1), spread[256 * column : 256 * column + 256, :])
         return total
 
     def coarse_solve():
@@ -439,32 +467,50 @@
         middle = 0.5 * (upper_edge + lower_edge)
         gap = 0.5 * (upper_edge - lower_edge)
         sigma = middle / gap
+        left_half = iota((64, 128), 1) < 64
+        halves = [slice(0, 64), slice(64, 128)]
+
+        def send(parity, half, direction):
+            high, rest = hi_lo(direction)
+            coarse_own[parity, halves[half], :] = jnp.where(left_half, high, rest)
+            begin(coarse_copies(parity, half))
+
         restrict()
-        d_now[...] = t_now[...] / middle[0:1, :]
-        z_now[...] = jnp.zeros((128, 128), F32)
-        left_half = iota((128, 128), 1) < 64
+        for half in range(2):
+            direction = t_now[halves[half], :] / middle[0:1, :]
+            send(0, half, direction)
+            d_now[halves[half], :] = direction
+            z_now[halves[half], :] = direction
 
         def step(number, rho):
             parity = lax.rem(number, 2)
-            direction = d_now[...]
-            high, rest = hi_lo(direction)
-            coarse_own[parity] = jnp.where(left_half, high, rest)
-            copies = coarse_copies(parity)
-            for copy in copies:
-                copy.start()
-            z_now[...] = z_now[...] + direction
-            for copy in copies:
-                copy.wait()
-            got = [coarse_own[parity]] + [coarse_got[parity, k] for k in range(4)]
-            coupled = coarse_product(got)
-            t_next = t_now[...] - live[...] * (cshift[...] * direction + coarse_speed * coupled)
-            t_now[...] = t_next
             rho_next = 1.0 / (2.0 * sigma - rho)
-            d_now[...] = (rho_next * rho)[0:1, :] * direction + (2.0 * rho_next / gap)[0:1, :] * t_next
+            for half in range(2):
+                rows = halves[half]
+                arrived(coarse_copies(parity, half))
+                got = [coarse_own[parity, rows, :]] + [coarse_got[parity, k, rows, :] for k in range(4)]
+                coupled = coarse_product(got)
+                direction = d_now[rows, :]
+                t_next = t_now[rows, :] - live[rows, :] * (cshift[rows, :] * direction + coarse_speed * coupled)
+                t_now[rows, :] = t_next
+                direction = (rho_next * rho)[0:1, :] * direction + (2.0 * rho_next / gap)[0:1, :] * t_next
+
+                @pl.when(jnp.logical_and(number > 0, number < CHEB - 2))
+                def _():
+                    departed(coarse_copies(1 - parity, half))
+
+                @pl.when(number < CHEB - 2)
+                def _():
+                    send(1 - parity, half, direction)
+
+                d_now[rows, :] = direction
+                z_now[rows, :] = z_now[rows, :] + direction
             return rho_next
 
         lax.fori_loop(0, CHEB - 1, step, 1.0 / sigma)
-        z_now[...] = z_now[...] + d_now[...]
+        for parity in range(2):
+            for half in range(2):
+                departed(coarse_copies(parity, half))
 
     def prolong(parity):
         following = 1 - parity
@@ -496,26 +542,22 @@
         @pl.when(number > 0)
         def _():
             operator_inner(parity)
-            copies = halo_copies(parity)
-            for copy in copies:
-                copy.wait()
             scale = jnp.where(number == 3, 0.0, 1.0)
             operator_outer(parity, scale)
+            for half in range(2):
+                departed(halo_copies(parity, half))
 
         @pl.when(number == 2)
         def _():
             bound_end(2)
             coarse_solve()
             prolong(parity)
+            for half in range(2):
+                begin(halo_copies(1 - parity, half))
 
         @pl.when(number != 2)
         def _():
-            smooth_step(parity)
-
-        @pl.when(number < 5)
-        def _():
-            for copy in halo_copies(1 - parity):
-                copy.start()
+            smooth_step(parity, number < 5)
 
         @pl.when(number == 0)
         def _():
@@ -551,7 +593,7 @@
 
 def local(stream_total, span_total, right_side, shift_fine, diag_blocks, smoother, couplings, coefficients,
           agg_ids, coarse_columns, coarse_blocks, coarse_shift):
-    columns = jnp.transpose(coarse_columns[0, 0], (1, 0))
+    columns = jnp.transpose(coarse_columns, (0, 3, 1, 2))[0]
     blocks = jnp.transpose(coarse_blocks[0, 0], (1, 0, 2))
     vm = pltpu.VMEM
     dma = pltpu.SemaphoreType.DMA
@@ -559,16 +601,16 @@
     shape = (PAIRS, ROWS, 128)
     scratch = [
         vm((8, 4, 64, 128), F32), vm((8, 64, 128), F32), vm((8, 64, 64, 128), BF), vm((8, 64, 64, 128), BF),
-        vm((8, 64, 64), BF), vm((8, 8, 128), F32), vm((8, 128), jnp.int32), vm((5, 32), jnp.int32),
+        vm((8, 64, 64), BF), vm((8, 8, 128), F32), vm((8, 128), jnp.int32), vm((5, 1, 32), jnp.int32),
         vm((5, 32, 4096), F32), vm((32, 64), F32),
         vm((PAIRS, 8192, 128), BF), vm((PAIRS, 8192, 128), BF), vm(shape, F32), vm(shape, F32), vm(shape, F32),
         vm(shape, F32), vm(shape, F32), vm(shape, F32), vm(shape, BF), vm((2, PAIRS + 2, WROWS, 128), BF),
         vm((8,) + shape, BF), vm((1024, 128), BF),
-        vm((128, 512), BF), vm((512, 128), BF), vm((4096, 128), BF), vm((5, 128, 128), BF), vm((128, 128), F32),
+        vm((128, 512), BF), vm((512, 128), BF), vm((4096, 128), BF), vm((5, 64, 64), BF), vm((128, 128), F32),
         vm((128, 128), F32), vm((128, 128), F32), vm((128, 128), F32), vm((128, 128), F32),
-        vm((2, 128, 128), BF), vm((2, 4, 128, 128), BF), vm((5, 128, 128), F32),
+        vm((2, 128, 128), BF), vm((2, 4, 128, 128), BF),
         vm((4, 8, 128), F32), vm((partners, 8, 128), F32), vm((128, 128), BF),
-        dma((16,)), dma((2, 4)), dma((2, 4)), dma((2, 4)), dma((2, 4)), dma((partners,)), dma((partners,)), dma((4,)),
+        dma((16,)), dma((2, 2, 3)), dma((2, 2, 3)), dma((2, 2, 4)), dma((2, 2, 4)), dma((partners,)), dma((partners,)), dma((4,)),
     ]
     anywhere = pl.BlockSpec(memory_space=pl.ANY)
     return pl.pallas_call(

time: 128 us -> 93.5 us (0.73)
  the two profiles are of different devices: /device:TPU:0 before, /device:TPU:24 now
where the time goes in v2:
time: 93.5 us; the launch traced here: 93.4 us
  Pallas kernels  91.1 us (97%)
  local copies, waits for them, and re-layouts  2.31 us (2%)
    pallas_call x1, Pallas kernels, local(): pl.pallas_call(functools.partial(kernel, stream_total, span_total), out_s...  91.1 us
    unnamed x1, local copies, waits for them, and re-layouts  2.31 us

profile of v2, /device:TPU:24, one launch (start us, length us, event | category | flops | bytes accessed | tf_op | source)
XLA Modules:
  0.0 93.4 jit_solution(8410636122631223575)
XLA Ops:
  0.0 91.1 %cycle.1 = f32[8,4,64,128]{3,2,1,0:T(8,128)} custom-call(f32[8,4,64,128]{3,2,1,0:T(8,128)} %rhs_hbm.1, f32[8,64,128]{2,1,0:T(8,128)} %shift_hbm.1, bf16[8,64,64,128]{3,2,1,0:T(8,128)(2,1)} %diag_hbm.1, bf16[8,64,64,128]{3,2,1,0:T(8,128)(2,1)} %smooth_hbm.1, bf16[8,64,64]{2,1,0:T(8,128)(2,1)} %couple_hbm.1, f32[8,8,128]{2,1,0:T(8,128)} %coef_hbm.1, ...), custom_call_target="tpu_custom_call" | custom-call | tf_op jit(solution)/shard_map/cycle/pallas_call | solution.py:616
  91.1 2.3 %copy.12 = f32[8,4,64,128]{3,2,1,0:T(8,128)} copy(f32[8,4,64,128]{3,2,1,0:T(8,128)} %cycle.1) | data formatting | bytes 2097152

commit v3 on v2

--- a/solution.py
+++ b/solution.py
@@ -14,6 +14,7 @@
 MESH = pl.DeviceIdType.MESH
 NT = (((1,), (1,)), ((), ()))
 PAIRS = 4
+QUADS = ((0, 3), (1, 2))
 ROWS = 512
 EDGE = 16
 WROWS = ROWS + 2 * EDGE
@@ -55,7 +56,7 @@
                 halves.append(jnp.where(is_even, even, jnp.where(is_odd, odd, none)))
             lines.append(jnp.concatenate(halves, 1))
     rows = pl.ds(pl.multiple_of(step * 256, 256), 256)
-    weights = jnp.concatenate([blocks[2 * quad, rows, :], blocks[2 * quad + 1, rows, :]], 1)
+    weights = jnp.concatenate([blocks[pair, rows, :] for pair in QUADS[quad]], 1)
     product = dot(jnp.concatenate(lines, 0), weights)
     results = []
     for half in range(2):
@@ -82,7 +83,7 @@
                 blocks[pair, pl.ds(place, 16), :] = cube[node]
         return carry
 
-    lax.fori_loop(0, 4, some_columns, 0)
+    lax.fori_loop(0, 4, some_columns, 0, unroll=2)
 
 
 def kernel(
@@ -93,8 +94,8 @@
     raw_rhs, raw_shift, raw_diag, raw_smooth, raw_couple, raw_coef, raw_ids, raw_cols, raw_coarse, raw_cshift,
     diag, smoother, rhs, shift, inverse, field, image, residual, low, wide, coef, couple,
     member, member_t, spread, pick, live, cshift, z_now, t_now, d_now, coarse_own, coarse_got,
-    bound, bound_got, idpad,
-    load_sem, halo_send, halo_recv, coarse_send, coarse_recv, bound_send, bound_recv, store_sem,
+    bound, bound_got, idpad, by_node,
+    load_sem, halo_send, halo_recv, span_send, span_recv, coarse_send, coarse_recv, bound_send, bound_recv, store_sem,
 ):
     position = lax.axis_index("stream")
     across = lax.axis_index("span")
@@ -193,31 +194,7 @@
     slot = (rows & 31).astype(F32)
     found = jnp.max(jnp.where(by_slot == slot, 1.0, 0.0), axis=1, keepdims=True)
     live[...] = jnp.broadcast_to(found, (128, 128))
-    by_slot = by_slot.astype(BF)
-    rows = iota((128, 512), 0)
-    lanes = iota((128, 512), 1)
-    node_of = one_zero(lax.shift_right_logical(lanes, 2) == rows)
-    wide_ids = dot(by_slot, node_of)
-    same = (lanes & 3) == lax.shift_right_logical(rows, 5)
-    member[...] = one_zero(jnp.logical_and(wide_ids == (rows & 31).astype(F32), same))
-    rows = iota((512, 128), 0)
-    lanes = iota((512, 128), 1)
-    of_node = one_zero(lax.shift_right_logical(rows, 2) == lanes)
-    tall_ids = dot_nt(of_node, by_slot)
-    same = (rows & 3) == lax.shift_right_logical(lanes, 5)
-    member_t[...] = one_zero(jnp.logical_and(tall_ids == (lanes & 31).astype(F32), same))
-
-    load_cols.wait()
-    rows = iota((64, 32), 0)
-    lanes = iota((64, 32), 1)
-    repeat_rows = one_zero((rows & 31) == lanes)
-    rows = iota((64, 64), 0)
-    lanes = iota((64, 64), 1)
-    same = lax.shift_right_logical(rows, 5) == lax.shift_right_logical(lanes, 5)
-    for number in range(5):
-        line = jnp.broadcast_to(raw_cols[number].astype(F32), (64, 32)).astype(BF)
-        column = dot_nt(repeat_rows, line)
-        pick[number] = one_zero(jnp.logical_and(column == (lanes & 31).astype(F32), same))
+    by_node[...] = by_slot.astype(BF)
 
     load_cshift.wait()
     twice = jnp.where((iota((64, 128), 1) & 63) == iota((64, 128), 0), 1.0, 0.0)
@@ -248,6 +225,34 @@
             coef[number, 2 * half] = laid[:, :128]
             coef[number, 2 * half + 1] = laid[:, 128:]
 
+    def member_table():
+        rows = iota((128, 512), 0)
+        lanes = iota((128, 512), 1)
+        node_of = one_zero(lax.shift_right_logical(lanes, 2) == rows)
+        wide_ids = dot(by_node[...], node_of)
+        same = (lanes & 3) == lax.shift_right_logical(rows, 5)
+        member[...] = one_zero(jnp.logical_and(wide_ids == (rows & 31).astype(F32), same))
+
+    def coarse_tables():
+        rows = iota((512, 128), 0)
+        lanes = iota((512, 128), 1)
+        of_node = one_zero(lax.shift_right_logical(rows, 2) == lanes)
+        tall_ids = dot_nt(of_node, by_node[...])
+        same = (rows & 3) == lax.shift_right_logical(lanes, 5)
+        member_t[...] = one_zero(jnp.logical_and(tall_ids == (lanes & 31).astype(F32), same))
+
+        load_cols.wait()
+        rows = iota((64, 32), 0)
+        lanes = iota((64, 32), 1)
+        repeat_rows = one_zero((rows & 31) == lanes)
+        rows = iota((64, 64), 0)
+        lanes = iota((64, 64), 1)
+        same = lax.shift_right_logical(rows, 5) == lax.shift_right_logical(lanes, 5)
+        for number in range(5):
+            line = jnp.broadcast_to(raw_cols[number].astype(F32), (64, 32)).astype(BF)
+            column = dot_nt(repeat_rows, line)
+            pick[number] = one_zero(jnp.logical_and(column == (lanes & 31).astype(F32), same))
+
     pl.semaphore_wait(barrier, len(greeted))
 
     bound_copies = [
@@ -307,52 +312,89 @@
         pl.when(position < stream_total - 1)(copies[0].wait_send)
         pl.when(position > 0)(copies[1].wait_send)
 
-    def halo_copies(parity, half):
-        def copy(number, source, target, who):
-            return pltpu.make_async_remote_copy(
-                src_ref=source,
-                dst_ref=target,
-                send_sem=halo_send.at[parity, half, number],
-                recv_sem=halo_recv.at[parity, half, number],
-                device_id=who,
-                device_id_type=MESH,
+    def halo_copy(source, target, send_sem, recv_sem, who):
+        return pltpu.make_async_remote_copy(
+            src_ref=source, dst_ref=target, send_sem=send_sem, recv_sem=recv_sem, device_id=who, device_id_type=MESH
+        )
+
+    def stream_copies(parity, half):
+        mine = pl.ds(pl.multiple_of(EDGE + half * (ROWS // 2), 16), ROWS // 2)
+        ends = [(PAIRS, 0, after), (1, PAIRS + 1, before)]
+        return [
+            halo_copy(
+                wide.at[parity, source, mine], wide.at[parity, target, mine],
+                halo_send.at[parity, half, number], halo_recv.at[parity, half, number], (who, across),
             )
-
-        mine = pl.ds(pl.multiple_of(EDGE + half * (ROWS // 2), 16), ROWS // 2)
+            for number, (source, target, who) in enumerate(ends)
+        ]
+
+    def span_copies(parity):
         inner = pl.ds(1, PAIRS)
-        edge = pl.ds(pl.multiple_of(EDGE + half * (ROWS - EDGE), 16), EDGE)
-        beyond = pl.ds(pl.multiple_of((1 - half) * (ROWS + EDGE), 16), EDGE)
-        beside = lax.rem(across + span_total - 1 + 2 * half, span_total)
+        ends = [(ROWS, 0, right), (EDGE, ROWS + EDGE, left)]
         return [
-            copy(0, wide.at[parity, PAIRS, mine], wide.at[parity, 0, mine], (after, across)),
-            copy(1, wide.at[parity, 1, mine], wide.at[parity, PAIRS + 1, mine], (before, across)),
-            copy(2, wide.at[parity, inner, edge], wide.at[parity, inner, beyond], (position, beside)),
+            halo_copy(
+                wide.at[parity, inner, pl.ds(source, EDGE)], wide.at[parity, inner, pl.ds(target, EDGE)],
+                span_send.at[parity, number], span_recv.at[parity, number], (position, who),
+            )
+            for number, (source, target, who) in enumerate(ends)
         ]
+
+    def span_begin(parity):
+        for copy in span_copies(parity):
+            copy.start()
+
+    def halo_departed(parity):
+        for half in range(2):
+            departed(stream_copies(parity, half))
+        for copy in span_copies(parity):
+            copy.wait_send()
+
+    def result_copy(pair):
+        return pltpu.make_async_copy(field.at[pair], out_hbm.at[pair], store_sem.at[pair])
 
     def smooth_step(parity, more):
         following = 1 - parity
 
-        def tiles(part, carry):
-            for inside in range(32):
-                quad, step = inside % 2, part * 16 + inside // 2
-                rows = pl.ds(pl.multiple_of(step * 16, 16), 16)
-                shifted = pl.ds(pl.multiple_of(step * 16 + EDGE, 16), 16)
-                operand = [low[2 * quad + half, rows, :] for half in range(2)]
-                parts = block_tile(smoother, operand, quad, step)
-                for half in range(2):
-                    pair = 2 * quad + half
-                    change = residual[pair, rows, :] * inverse[pair, rows, :] + parts[half]
-                    value = field[pair, rows, :] + OMEGA * change
-                    field[pair, rows, :] = value
-                    wide[following, pair + 1, shifted, :] = value.astype(BF)
+        def tile(quad, step):
+            rows = pl.ds(pl.multiple_of(step * 16, 16), 16)
+            shifted = pl.ds(pl.multiple_of(step * 16 + EDGE, 16), 16)
+            parts = block_tile(smoother, [low[pair, rows, :] for pair in QUADS[quad]], quad, step)
+            for pair, part in zip(QUADS[quad], parts):
+                change = residual[pair, rows, :] * inverse[pair, rows, :] + part
+                value = field[pair, rows, :] + OMEGA * change
+                field[pair, rows, :] = value
+                wide[following, pair + 1, shifted, :] = value.astype(BF)
+
+        def outside(half, carry):
+            for inside in range(16):
+                tile(0, half * 16 + inside)
 
             @pl.when(more)
             def _():
-                begin(halo_copies(following, part))
+                begin(stream_copies(following, half))
 
             return carry
 
-        lax.fori_loop(0, 2, tiles, 0)
+        def inside_of(half, carry):
+            for inside in range(15):
+                tile(1, half * 15 + 1 + inside)
+            return carry
+
+        lax.fori_loop(0, 2, outside, 0)
+
+        @pl.when(jnp.logical_not(more))
+        def _():
+            for pair in QUADS[0]:
+                result_copy(pair).start()
+
+        for step in (0, 31):
+            tile(1, step)
+
+        @pl.when(more)
+        def _():
+            span_begin(following)
+
+        lax.fori_loop(0, 2, inside_of, 0)
 
     def operator_inner(parity):
         def tiles(part, carry):
@@ -360,35 +402,33 @@
                 quad, step = inside % 2, part * 16 + inside // 2
                 rows = pl.ds(pl.multiple_of(step * 16, 16), 16)
                 shifted = pl.ds(pl.multiple_of(step * 16 + EDGE, 16), 16)
-                operand = [wide[parity, 2 * quad + half + 1, shifted, :] for half in range(2)]
+                operand = [wide[parity, pair + 1, shifted, :] for pair in QUADS[quad]]
                 parts = block_tile(diag, operand, quad, step)
-                for half in range(2):
-                    pair = 2 * quad + half
-                    image[pair, rows, :] = shift[pair, rows, :] * operand[half].astype(F32) + parts[half]
+                for pair, value, part_of in zip(QUADS[quad], operand, parts):
+                    image[pair, rows, :] = shift[pair, rows, :] * value.astype(F32) + part_of
             return carry
 
         lax.fori_loop(0, 2, tiles, 0)
 
     def operator_outer(parity, scale):
-        left_half = iota((128, 128), 1) < 64
-
-        def chunk(pair, start):
-            rows = pl.ds(pl.multiple_of(start, 128), 128)
+        def chunk(pair, start, size):
+            left_half = iota((size, 128), 1) < 64
+            rows = pl.ds(pl.multiple_of(start, 128), size)
 
             def at(which):
-                return wide[parity, which, pl.ds(pl.multiple_of(start + EDGE, 16), 128), :]
+                return wide[parity, which, pl.ds(pl.multiple_of(start + EDGE, 16), size), :]
 
             here_now, lower, upper = at(pair + 1), at(pair), at(pair + 2)
-            around = wide[parity, pair + 1, pl.ds(pl.multiple_of(start, 16), 128 + 2 * EDGE), :]
+            around = wide[parity, pair + 1, pl.ds(pl.multiple_of(start, 16), size + 2 * EDGE), :]
             shifted = [
                 lower,
                 pltpu.roll(jnp.where(left_half, here_now, lower).astype(F32), 64, 1).astype(BF),
                 pltpu.roll(jnp.where(left_half, upper, here_now).astype(F32), 64, 1).astype(BF),
                 upper,
-                around[EDGE - 8 : EDGE + 120],
-                around[EDGE - 4 : EDGE + 124],
-                around[EDGE + 4 : EDGE + 132],
-                around[EDGE + 8 : EDGE + 136],
+                around[EDGE - 8 : EDGE - 8 + size],
+                around[EDGE - 4 : EDGE - 4 + size],
+                around[EDGE + 4 : EDGE + 4 + size],
+                around[EDGE + 8 : EDGE + 8 + size],
             ]
             operand = jnp.concatenate([coef[m, pair, rows, :] * shifted[m] for m in range(8)], 1)
             value = scale * rhs[pair, rows, :] - (image[pair, rows, :] + dot(operand, couple[...]))
@@ -396,19 +436,21 @@
             low[pair, rows, :] = value.astype(BF)
 
         for pair in (1, 2):
-            for start in (128, 256):
-                chunk(pair, start)
+            chunk(pair, 128, 256)
+        for copy in span_copies(parity):
+            copy.wait_recv()
+        for pair in (1, 2):
+            for start in (0, 384):
+                chunk(pair, start, 128)
         for half in range(2):
-            arrived(halo_copies(parity, half))
-
-        def chunks(number, carry):
-            mixed = number // 2
-            for inside in range(4):
-                pair = mixed * (1 + inside // 2) + (1 - mixed) * 3 * number
-                chunk(pair, 128 * (mixed * 3 * (inside % 2) + (1 - mixed) * inside))
+            arrived(stream_copies(parity, half))
+
+        def outer_pairs(number, carry):
+            for start in (0, 256):
+                chunk(3 * number, start, 256)
             return carry
 
-        lax.fori_loop(0, 3, chunks, 0)
+        lax.fori_loop(0, 2, outer_pairs, 0)
 
     def coarse_copies(parity, half):
         targets = [(after, across), (before, across), (position, right), (position, left)]
@@ -481,6 +523,7 @@
             send(0, half, direction)
             d_now[halves[half], :] = direction
             z_now[halves[half], :] = direction
+        coarse_tables()
 
         def step(number, rho):
             parity = lax.rem(number, 2)
@@ -536,16 +579,14 @@
             for pair in range(PAIRS):
                 load_smooth[pair].wait()
                 relayout(raw_smooth, smoother, pair)
-            coarse_bound()
-            bound_begin(0)
 
         @pl.when(number > 0)
         def _():
             operator_inner(parity)
+            pl.when(number == 2)(member_table)
             scale = jnp.where(number == 3, 0.0, 1.0)
             operator_outer(parity, scale)
-            for half in range(2):
-                departed(halo_copies(parity, half))
+            halo_departed(parity)
 
         @pl.when(number == 2)
         def _():
@@ -553,7 +594,8 @@
             coarse_solve()
             prolong(parity)
             for half in range(2):
-                begin(halo_copies(1 - parity, half))
+                begin(stream_copies(1 - parity, half))
+            span_begin(1 - parity)
 
         @pl.when(number != 2)
         def _():
@@ -561,11 +603,13 @@
 
         @pl.when(number == 0)
         def _():
-            bound_end(0)
-            bound_begin(1)
+            coarse_bound()
+            bound_begin(0)
             for pair in range(PAIRS):
                 load_diag[pair].wait()
                 relayout(raw_diag, diag, pair)
+            bound_end(0)
+            bound_begin(1)
 
         @pl.when(number == 1)
         def _():
@@ -576,19 +620,29 @@
 
     lax.fori_loop(0, 6, round_of, 0)
 
-    stores = []
+    for pair in QUADS[1]:
+        result_copy(pair).start()
     for pair in range(PAIRS):
+        result_copy(pair).wait()
+
+
+def unfold(field_hbm, out_hbm, field, out, load_sem, store_sem):
+    loads = [pltpu.make_async_copy(field_hbm.at[pair], field.at[pair], load_sem.at[pair]) for pair in range(PAIRS)]
+    stores = [
+        pltpu.make_async_copy(out.at[pl.ds(2 * pair, 2)], out_hbm.at[pl.ds(2 * pair, 2)], store_sem.at[pair])
+        for pair in range(PAIRS)
+    ]
+    for load in loads:
+        load.start()
+    for pair in range(PAIRS):
+        loads[pair].wait()
         for vector in range(4):
             block = field[pair, pl.ds(vector, 128, stride=4), :].T
-            raw_rhs[2 * pair, vector] = block[0:64]
-            raw_rhs[2 * pair + 1, vector] = block[64:128]
-        copy = pltpu.make_async_copy(
-            raw_rhs.at[pl.ds(2 * pair, 2)], out_hbm.at[pl.ds(2 * pair, 2)], store_sem.at[pair]
-        )
-        copy.start()
-        stores.append(copy)
-    for copy in stores:
-        copy.wait()
+            out[2 * pair, vector] = block[0:64]
+            out[2 * pair + 1, vector] = block[64:128]
+        stores[pair].start()
+    for store in stores:
+        store.wait()
 
 
 def local(stream_total, span_total, right_side, shift_fine, diag_blocks, smoother, couplings, coefficients,
@@ -609,13 +663,13 @@
         vm((128, 512), BF), vm((512, 128), BF), vm((4096, 128), BF), vm((5, 64, 64), BF), vm((128, 128), F32),
         vm((128, 128), F32), vm((128, 128), F32), vm((128, 128), F32), vm((128, 128), F32),
         vm((2, 128, 128), BF), vm((2, 4, 128, 128), BF),
-        vm((4, 8, 128), F32), vm((partners, 8, 128), F32), vm((128, 128), BF),
-        dma((16,)), dma((2, 2, 3)), dma((2, 2, 3)), dma((2, 2, 4)), dma((2, 2, 4)), dma((partners,)), dma((partners,)), dma((4,)),
+        vm((4, 8, 128), F32), vm((partners, 8, 128), F32), vm((128, 128), BF), vm((128, 128), BF),
+        dma((16,)), dma((2, 2, 2)), dma((2, 2, 2)), dma((2, 2)), dma((2, 2)), dma((2, 2, 4)), dma((2, 2, 4)), dma((partners,)), dma((partners,)), dma((4,)),
     ]
     anywhere = pl.BlockSpec(memory_space=pl.ANY)
-    return pl.pallas_call(
+    result = pl.pallas_call(
         functools.partial(kernel, stream_total, span_total),
-        out_shape=jax.ShapeDtypeStruct(right_side.shape, F32),
+        out_shape=jax.ShapeDtypeStruct(shape, F32),
         in_specs=[anywhere] * 10,
         out_specs=anywhere,
         scratch_shapes=scratch,
@@ -625,6 +679,15 @@
         name="cycle",
     )(right_side, shift_fine, diag_blocks, smoother, couplings, coefficients, agg_ids, columns, blocks,
       coarse_shift[0, 0])
+    return pl.pallas_call(
+        unfold,
+        out_shape=jax.ShapeDtypeStruct(right_side.shape, F32),
+        in_specs=[anywhere],
+        out_specs=anywhere,
+        scratch_shapes=[vm(shape, F32), vm((8, 4, 64, 128), F32), dma((PAIRS,)), dma((PAIRS,))],
+        compiler_params=pltpu.CompilerParams(vmem_limit_bytes=60 * 1024 * 1024),
+        name="unfold",
+    )(result)
 
 
 def solution(mesh):

time: 93.5 us -> 87.8 us (0.939)
  the two profiles are of different devices: /device:TPU:24 before, /device:TPU:0 now
where the time goes in v3:
time: 87.8 us; the launch traced here: 87.2 us
  Pallas kernels  87 us (99%)
    pallas_call x1, Pallas kernels, local(): pl.pallas_call(functools.partial(kernel, stream_total, span_total), out_s...  84.8 us
    pallas_call x1, Pallas kernels, local(): pl.pallas_call(unfold, out_shape=jax.ShapeDtypeStruct(right_side.shape, F...  2.26 us

profile of v3, /device:TPU:0, one launch (start us, length us, event | category | flops | bytes accessed | tf_op | source)
XLA Modules:
  0.0 87.2 jit_solution(6192896329565218481)
XLA Ops:
  0.0 84.8 %cycle.1.field_hbm = f32[4,512,128]{2,1,0:T(8,128)} custom-call(f32[8,4,64,128]{3,2,1,0:T(8,128)} %rhs_hbm.1, f32[8,64,128]{2,1,0:T(8,128)} %shift_hbm.1, bf16[8,64,64,128]{3,2,1,0:T(8,128)(2,1)} %diag_hbm.1, bf16[8,64,64,128]{3,2,1,0:T(8,128)(2,1)} %smooth_hbm.1, bf16[8,64,64]{2,1,0:T(8,128)(2,1)} %couple_hbm.1, f32[8,8,128]{2,1,0:T(8,128)} %coef_hbm.1, ...), custom_call_target="tpu_custom_call" | custom-call | tf_op jit(solution)/shard_map/cycle/pallas_call | solution.py:670
  84.8 2.3 %unfold.1 = f32[8,4,64,128]{3,2,1,0:T(8,128)} custom-call(f32[4,512,128]{2,1,0:T(8,128)} %cycle.1.field_hbm), custom_call_target="tpu_custom_call" | custom-call | tf_op jit(solution)/shard_map/unfold/pallas_call | solution.py:682

commit v4 on v3

--- a/solution.py
+++ b/solution.py
@@ -55,7 +55,7 @@
                 is_odd = jnp.logical_and(node == 2 * part + 1, jnp.logical_not(left))
                 halves.append(jnp.where(is_even, even, jnp.where(is_odd, odd, none)))
             lines.append(jnp.concatenate(halves, 1))
-    rows = pl.ds(pl.multiple_of(step * 256, 256), 256)
+    rows = pl.ds(step * 256, 256)
     weights = jnp.concatenate([blocks[pair, rows, :] for pair in QUADS[quad]], 1)
     product = dot(jnp.concatenate(lines, 0), weights)
     results = []
@@ -95,7 +95,7 @@
     diag, smoother, rhs, shift, inverse, field, image, residual, low, wide, coef, couple,
     member, member_t, spread, pick, live, cshift, z_now, t_now, d_now, coarse_own, coarse_got,
     bound, bound_got, idpad, by_node,
-    load_sem, halo_send, halo_recv, span_send, span_recv, coarse_send, coarse_recv, bound_send, bound_recv, store_sem,
+    load_sem, halo_send, halo_recv, coarse_send, coarse_recv, bound_send, bound_recv, store_sem,
 ):
     position = lax.axis_index("stream")
     across = lax.axis_index("span")
@@ -242,16 +242,11 @@
         member_t[...] = one_zero(jnp.logical_and(tall_ids == (lanes & 31).astype(F32), same))
 
         load_cols.wait()
-        rows = iota((64, 32), 0)
-        lanes = iota((64, 32), 1)
-        repeat_rows = one_zero((rows & 31) == lanes)
-        rows = iota((64, 64), 0)
-        lanes = iota((64, 64), 1)
-        same = lax.shift_right_logical(rows, 5) == lax.shift_right_logical(lanes, 5)
+        repeat_rows = one_zero(iota((32, 32), 0) == iota((32, 32), 1))
+        lanes = iota((32, 32), 1).astype(F32)
         for number in range(5):
-            line = jnp.broadcast_to(raw_cols[number].astype(F32), (64, 32)).astype(BF)
-            column = dot_nt(repeat_rows, line)
-            pick[number] = one_zero(jnp.logical_and(column == (lanes & 31).astype(F32), same))
+            line = jnp.broadcast_to(raw_cols[number].astype(F32), (32, 32)).astype(BF)
+            pick[number] = one_zero(dot_nt(repeat_rows, line) == lanes)
 
     pl.semaphore_wait(barrier, len(greeted))
 
@@ -317,100 +312,82 @@
             src_ref=source, dst_ref=target, send_sem=send_sem, recv_sem=recv_sem, device_id=who, device_id_type=MESH
         )
 
-    def stream_copies(parity, half):
-        mine = pl.ds(pl.multiple_of(EDGE + half * (ROWS // 2), 16), ROWS // 2)
+    def stream_copies(parity, first, start, size):
+        mine = pl.ds(EDGE + start, size)
         ends = [(PAIRS, 0, after), (1, PAIRS + 1, before)]
         return [
             halo_copy(
                 wide.at[parity, source, mine], wide.at[parity, target, mine],
-                halo_send.at[parity, half, number], halo_recv.at[parity, half, number], (who, across),
+                halo_send.at[parity, first + number], halo_recv.at[parity, first + number], (who, across),
             )
             for number, (source, target, who) in enumerate(ends)
         ]
 
-    def span_copies(parity):
-        inner = pl.ds(1, PAIRS)
+    def span_copies(parity, first, low_pair, count):
+        pairs = pl.ds(low_pair + 1, count)
         ends = [(ROWS, 0, right), (EDGE, ROWS + EDGE, left)]
         return [
             halo_copy(
-                wide.at[parity, inner, pl.ds(source, EDGE)], wide.at[parity, inner, pl.ds(target, EDGE)],
-                span_send.at[parity, number], span_recv.at[parity, number], (position, who),
+                wide.at[parity, pairs, pl.ds(source, EDGE)], wide.at[parity, pairs, pl.ds(target, EDGE)],
+                halo_send.at[parity, first + number], halo_recv.at[parity, first + number], (position, who),
             )
             for number, (source, target, who) in enumerate(ends)
         ]
 
-    def span_begin(parity):
-        for copy in span_copies(parity):
+    def middle_halo(parity):
+        return [], span_copies(parity, 0, 1, 2)
+
+    def edge_halo(parity):
+        return (
+            [stream_copies(parity, 2, 0, 128), stream_copies(parity, 4, 384, 128)],
+            span_copies(parity, 6, 0, 1) + span_copies(parity, 8, 3, 1),
+        )
+
+    def core_halo(parity):
+        return [stream_copies(parity, 10, 128, 256)], []
+
+    def halo_begin(halo):
+        for copies in halo[0]:
+            begin(copies)
+        for copy in halo[1]:
             copy.start()
 
-    def halo_departed(parity):
-        for half in range(2):
-            departed(stream_copies(parity, half))
-        for copy in span_copies(parity):
+    def halo_arrived(halo):
+        for copies in halo[0]:
+            arrived(copies)
+        for copy in halo[1]:
+            copy.wait_recv()
+
+    def halo_departed(halo):
+        for copies in halo[0]:
+            departed(copies)
+        for copy in halo[1]:
             copy.wait_send()
 
     def result_copy(pair):
         return pltpu.make_async_copy(field.at[pair], out_hbm.at[pair], store_sem.at[pair])
 
-    def smooth_step(parity, more):
+    def smooth_tiles(parity, quad, steps):
         following = 1 - parity
-
-        def tile(quad, step):
-            rows = pl.ds(pl.multiple_of(step * 16, 16), 16)
-            shifted = pl.ds(pl.multiple_of(step * 16 + EDGE, 16), 16)
+        for step in steps:
+            rows = pl.ds(step * 16, 16)
             parts = block_tile(smoother, [low[pair, rows, :] for pair in QUADS[quad]], quad, step)
             for pair, part in zip(QUADS[quad], parts):
                 change = residual[pair, rows, :] * inverse[pair, rows, :] + part
                 value = field[pair, rows, :] + OMEGA * change
                 field[pair, rows, :] = value
-                wide[following, pair + 1, shifted, :] = value.astype(BF)
-
-        def outside(half, carry):
-            for inside in range(16):
-                tile(0, half * 16 + inside)
-
-            @pl.when(more)
-            def _():
-                begin(stream_copies(following, half))
-
-            return carry
-
-        def inside_of(half, carry):
-            for inside in range(15):
-                tile(1, half * 15 + 1 + inside)
-            return carry
-
-        lax.fori_loop(0, 2, outside, 0)
-
-        @pl.when(jnp.logical_not(more))
-        def _():
-            for pair in QUADS[0]:
-                result_copy(pair).start()
-
-        for step in (0, 31):
-            tile(1, step)
-
-        @pl.when(more)
-        def _():
-            span_begin(following)
-
-        lax.fori_loop(0, 2, inside_of, 0)
+                wide[following, pair + 1, pl.ds(step * 16 + EDGE, 16), :] = value.astype(BF)
 
     def operator_inner(parity):
-        def tiles(part, carry):
-            for inside in range(32):
-                quad, step = inside % 2, part * 16 + inside // 2
-                rows = pl.ds(pl.multiple_of(step * 16, 16), 16)
-                shifted = pl.ds(pl.multiple_of(step * 16 + EDGE, 16), 16)
-                operand = [wide[parity, pair + 1, shifted, :] for pair in QUADS[quad]]
-                parts = block_tile(diag, operand, quad, step)
-                for pair, value, part_of in zip(QUADS[quad], operand, parts):
-                    image[pair, rows, :] = shift[pair, rows, :] * value.astype(F32) + part_of
-            return carry
-
-        lax.fori_loop(0, 2, tiles, 0)
-
-    def operator_outer(parity, scale):
+        for inside in range(64):
+            quad, step = inside % 2, inside // 2
+            rows = pl.ds(step * 16, 16)
+            operand = [wide[parity, pair + 1, pl.ds(step * 16 + EDGE, 16), :] for pair in QUADS[quad]]
+            parts = block_tile(diag, operand, quad, step)
+            for pair, value, part in zip(QUADS[quad], operand, parts):
+                image[pair, rows, :] = shift[pair, rows, :] * value.astype(F32) + part
+
+    def stencil(parity, scale):
         def chunk(pair, start, size):
             left_half = iota((size, 128), 1) < 64
             rows = pl.ds(pl.multiple_of(start, 128), size)
@@ -435,32 +412,17 @@
             residual[pair, rows, :] = value
             low[pair, rows, :] = value.astype(BF)
 
-        for pair in (1, 2):
-            chunk(pair, 128, 256)
-        for copy in span_copies(parity):
-            copy.wait_recv()
-        for pair in (1, 2):
-            for start in (0, 384):
-                chunk(pair, start, 128)
-        for half in range(2):
-            arrived(stream_copies(parity, half))
-
-        def outer_pairs(number, carry):
-            for start in (0, 256):
-                chunk(3 * number, start, 256)
-            return carry
-
-        lax.fori_loop(0, 2, outer_pairs, 0)
-
-    def coarse_copies(parity, half):
+        return chunk
+
+    def coarse_copies(parity, vector):
         targets = [(after, across), (before, across), (position, right), (position, left)]
-        rows = pl.ds(64 * half, 64)
+        rows = pl.ds(32 * vector, 32)
         return [
             pltpu.make_async_remote_copy(
                 src_ref=coarse_own.at[parity, rows],
                 dst_ref=coarse_got.at[parity, number, rows],
-                send_sem=coarse_send.at[parity, half, number],
-                recv_sem=coarse_recv.at[parity, half, number],
+                send_sem=coarse_send.at[parity, vector, number],
+                recv_sem=coarse_recv.at[parity, vector, number],
                 device_id=who,
                 device_id_type=MESH,
             )
@@ -486,20 +448,16 @@
         for number in range(5):
             value = dot(pick[number], got[number])
             near.append(value + pltpu.roll(value, 64, 1))
-        total = jnp.zeros((64, 128), F32)
+        total = jnp.zeros((32, 128), F32)
         for column in range(16):
             sides = []
             for side in range(2):
                 begin_at = 256 * column + 128 * side
                 blocks = [raw_coarse[k, :, begin_at : begin_at + 128] for k in range(5)]
-                pieces = []
-                for vector in range(2):
-                    rows = slice(32 * vector, 32 * vector + 32)
-                    part = blocks[0] * near[0][rows]
-                    for k in range(1, 5):
-                        part = part + blocks[k] * near[k][rows]
-                    pieces.append(part.astype(BF))
-                sides.append(jnp.concatenate(pieces, 0))
+                part = blocks[0] * near[0]
+                for k in range(1, 5):
+                    part = part + blocks[k] * near[k]
+                sides.append(part.astype(BF))
             total = total + dot(jnp.concatenate(sides, 1), spread[256 * column : 256 * column + 256, :])
         return total
 
@@ -509,28 +467,28 @@
         middle = 0.5 * (upper_edge + lower_edge)
         gap = 0.5 * (upper_edge - lower_edge)
         sigma = middle / gap
-        left_half = iota((64, 128), 1) < 64
-        halves = [slice(0, 64), slice(64, 128)]
-
-        def send(parity, half, direction):
+        left_half = iota((32, 128), 1) < 64
+        vectors = [slice(32 * vector, 32 * vector + 32) for vector in range(4)]
+
+        def send(parity, vector, direction):
             high, rest = hi_lo(direction)
-            coarse_own[parity, halves[half], :] = jnp.where(left_half, high, rest)
-            begin(coarse_copies(parity, half))
+            coarse_own[parity, vectors[vector], :] = jnp.where(left_half, high, rest)
+            begin(coarse_copies(parity, vector))
 
         restrict()
-        for half in range(2):
-            direction = t_now[halves[half], :] / middle[0:1, :]
-            send(0, half, direction)
-            d_now[halves[half], :] = direction
-            z_now[halves[half], :] = direction
+        for vector in range(4):
+            direction = t_now[vectors[vector], :] / middle[0:1, :]
+            send(0, vector, direction)
+            d_now[vectors[vector], :] = direction
+            z_now[vectors[vector], :] = direction
         coarse_tables()
 
         def step(number, rho):
             parity = lax.rem(number, 2)
             rho_next = 1.0 / (2.0 * sigma - rho)
-            for half in range(2):
-                rows = halves[half]
-                arrived(coarse_copies(parity, half))
+            for vector in range(4):
+                rows = vectors[vector]
+                arrived(coarse_copies(parity, vector))
                 got = [coarse_own[parity, rows, :]] + [coarse_got[parity, k, rows, :] for k in range(4)]
                 coupled = coarse_product(got)
                 direction = d_now[rows, :]
@@ -540,11 +498,11 @@
 
                 @pl.when(jnp.logical_and(number > 0, number < CHEB - 2))
                 def _():
-                    departed(coarse_copies(1 - parity, half))
+                    departed(coarse_copies(1 - parity, vector))
 
                 @pl.when(number < CHEB - 2)
                 def _():
-                    send(1 - parity, half, direction)
+                    send(1 - parity, vector, direction)
 
                 d_now[rows, :] = direction
                 z_now[rows, :] = z_now[rows, :] + direction
@@ -552,8 +510,8 @@
 
         lax.fori_loop(0, CHEB - 1, step, 1.0 / sigma)
         for parity in range(2):
-            for half in range(2):
-                departed(coarse_copies(parity, half))
+            for vector in range(4):
+                departed(coarse_copies(parity, vector))
 
     def prolong(parity):
         following = 1 - parity
@@ -580,26 +538,71 @@
                 load_smooth[pair].wait()
                 relayout(raw_smooth, smoother, pair)
 
+        following = 1 - parity
+        more = number < 5
+        chunk = stencil(parity, jnp.where(number == 3, 0.0, 1.0))
+        ends = (0, 384)
+
         @pl.when(number > 0)
         def _():
             operator_inner(parity)
             pl.when(number == 2)(member_table)
-            scale = jnp.where(number == 3, 0.0, 1.0)
-            operator_outer(parity, scale)
-            halo_departed(parity)
+            for pair in QUADS[1]:
+                chunk(pair, 128, 256)
+            halo_arrived(middle_halo(parity))
+            for pair in QUADS[1]:
+                for start in ends:
+                    chunk(pair, start, 128)
+
+        @pl.when(number != 2)
+        def _():
+            smooth_tiles(parity, 1, (0, 31))
+            pl.when(more)(lambda: halo_begin(middle_halo(following)))
+
+        @pl.when(number > 0)
+        def _():
+            halo_arrived(edge_halo(parity))
+            for pair in QUADS[0]:
+                for start in ends:
+                    chunk(pair, start, 128)
+
+        @pl.when(number != 2)
+        def _():
+            smooth_tiles(parity, 0, [*range(8), *range(24, 32)])
+            pl.when(more)(lambda: halo_begin(edge_halo(following)))
+
+        @pl.when(number > 0)
+        def _():
+            halo_arrived(core_halo(parity))
+            for pair in QUADS[0]:
+                chunk(pair, 128, 256)
+
+        @pl.when(number != 2)
+        def _():
+            smooth_tiles(parity, 0, range(8, 24))
+            pl.when(more)(lambda: halo_begin(core_halo(following)))
 
         @pl.when(number == 2)
         def _():
             bound_end(2)
             coarse_solve()
             prolong(parity)
-            for half in range(2):
-                begin(stream_copies(1 - parity, half))
-            span_begin(1 - parity)
+            for halo in (middle_halo, edge_halo, core_halo):
+                halo_begin(halo(following))
+
+        @pl.when(number == 5)
+        def _():
+            for pair in QUADS[0]:
+                result_copy(pair).start()
 
         @pl.when(number != 2)
         def _():
-            smooth_step(parity, number < 5)
+            smooth_tiles(parity, 1, range(1, 31))
+
+        @pl.when(number > 0)
+        def _():
+            for halo in (middle_halo, edge_halo, core_halo):
+                halo_departed(halo(parity))
 
         @pl.when(number == 0)
         def _():
@@ -660,11 +663,11 @@
         vm((PAIRS, 8192, 128), BF), vm((PAIRS, 8192, 128), BF), vm(shape, F32), vm(shape, F32), vm(shape, F32),
         vm(shape, F32), vm(shape, F32), vm(shape, F32), vm(shape, BF), vm((2, PAIRS + 2, WROWS, 128), BF),
         vm((8,) + shape, BF), vm((1024, 128), BF),
-        vm((128, 512), BF), vm((512, 128), BF), vm((4096, 128), BF), vm((5, 64, 64), BF), vm((128, 128), F32),
+        vm((128, 512), BF), vm((512, 128), BF), vm((4096, 128), BF), vm((5, 32, 32), BF), vm((128, 128), F32),
         vm((128, 128), F32), vm((128, 128), F32), vm((128, 128), F32), vm((128, 128), F32),
         vm((2, 128, 128), BF), vm((2, 4, 128, 128), BF),
         vm((4, 8, 128), F32), vm((partners, 8, 128), F32), vm((128, 128), BF), vm((128, 128), BF),
-        dma((16,)), dma((2, 2, 2)), dma((2, 2, 2)), dma((2, 2)), dma((2, 2)), dma((2, 2, 4)), dma((2, 2, 4)), dma((partners,)), dma((partners,)), dma((4,)),
+        dma((16,)), dma((2, 12)), dma((2, 12)), dma((2, 4, 4)), dma((2, 4, 4)), dma((partners,)), dma((partners,)), dma((4,)),
     ]
     anywhere = pl.BlockSpec(memory_space=pl.ANY)
     result = pl.pallas_call(

time: 87.8 us -> 85.2 us (0.970)
  Pallas kernels: 87 us -> 84.4 us
    pallas_call x1, Pallas kernels: 84.8 us -> 82.1 us  [local(): pl.pallas_call(functools.partial(kernel, stream_total, span_total), out_s...]
where the time goes in v4:
time: 85.2 us; the launch traced here: 84.5 us
  Pallas kernels  84.4 us (99%)
    pallas_call x1, Pallas kernels, local(): pl.pallas_call(functools.partial(kernel, stream_total, span_total), out_s...  82.1 us
    pallas_call x1, Pallas kernels, local(): pl.pallas_call(unfold, out_shape=jax.ShapeDtypeStruct(right_side.shape, F...  2.26 us

profile of v4, /device:TPU:0, one launch (start us, length us, event | category | flops | bytes accessed | tf_op | source)
XLA Modules:
  0.0 84.5 jit_solution(12076174839068067075)
XLA Ops:
  0.0 82.1 %cycle.1.field_hbm = f32[4,512,128]{2,1,0:T(8,128)} custom-call(f32[8,4,64,128]{3,2,1,0:T(8,128)} %rhs_hbm.1, f32[8,64,128]{2,1,0:T(8,128)} %shift_hbm.1, bf16[8,64,64,128]{3,2,1,0:T(8,128)(2,1)} %diag_hbm.1, bf16[8,64,64,128]{3,2,1,0:T(8,128)(2,1)} %smooth_hbm.1, bf16[8,64,64]{2,1,0:T(8,128)(2,1)} %couple_hbm.1, f32[8,8,128]{2,1,0:T(8,128)} %coef_hbm.1, ...), custom_call_target="tpu_custom_call" | custom-call | tf_op jit(solution)/shard_map/cycle/pallas_call | solution.py:673
  82.1 2.3 %unfold.1 = f32[8,4,64,128]{3,2,1,0:T(8,128)} custom-call(f32[4,512,128]{2,1,0:T(8,128)} %cycle.1.field_hbm), custom_call_target="tpu_custom_call" | custom-call | tf_op jit(solution)/shard_map/unfold/pallas_call | solution.py:685

commit v5 on v4

--- a/solution.py
+++ b/solution.py
@@ -83,7 +83,7 @@
                 blocks[pair, pl.ds(place, 16), :] = cube[node]
         return carry
 
-    lax.fori_loop(0, 4, some_columns, 0, unroll=2)
+    lax.fori_loop(0, 4, some_columns, 0, unroll=4)
 
 
 def kernel(
@@ -117,22 +117,6 @@
     partners = [who for stage in stages for who in stage]
     greeted = partners + [(after, across), (before, across)]
 
-    @pl.when(position == 0)
-    def _():
-        for parity in range(2):
-            wide[parity, 0] = jnp.zeros((WROWS, 128), BF)
-            coarse_got[parity, 0] = jnp.zeros((128, 128), BF)
-
-    @pl.when(position == stream_total - 1)
-    def _():
-        for parity in range(2):
-            wide[parity, PAIRS + 1] = jnp.zeros((WROWS, 128), BF)
-            coarse_got[parity, 1] = jnp.zeros((128, 128), BF)
-
-    barrier = pltpu.get_barrier_semaphore()
-    for who in greeted:
-        pl.semaphore_signal(barrier, inc=1, device_id=who, device_id_type=MESH)
-
     loads = []
 
     def load(source, target):
@@ -153,6 +137,22 @@
     ]
     load_coarse = load(coarse_hbm, raw_coarse)
     load_diag = [load(diag_hbm.at[pl.ds(2 * pair, 2)], raw_diag.at[pl.ds(2 * pair, 2)]) for pair in range(PAIRS)]
+
+    @pl.when(position == 0)
+    def _():
+        for parity in range(2):
+            wide[parity, 0] = jnp.zeros((WROWS, 128), BF)
+            coarse_got[parity, 0] = jnp.zeros((128, 128), BF)
+
+    @pl.when(position == stream_total - 1)
+    def _():
+        for parity in range(2):
+            wide[parity, PAIRS + 1] = jnp.zeros((WROWS, 128), BF)
+            coarse_got[parity, 1] = jnp.zeros((128, 128), BF)
+
+    barrier = pltpu.get_barrier_semaphore()
+    for who in greeted:
+        pl.semaphore_signal(barrier, inc=1, device_id=who, device_id_type=MESH)
 
     def speed_of(place, extent):
         return jnp.sqrt(1.0 + 8.0 * (place + 0.5) / extent)
@@ -518,11 +518,15 @@
         slots = lax.shift_right_logical(iota((128, 128), 0) & 31, 2)
         half = lax.shift_right_logical(iota((128, 128), 1), 6)
         twice = jnp.concatenate([member_t[...], member_t[...]], 1)
-        for pair in range(PAIRS):
+        for pair in (*QUADS[0], *QUADS[1]):
             high, rest = hi_lo(jnp.where(slots == 2 * pair + half, z_now[...], 0.0))
             value = dot(twice, jnp.concatenate([high, rest], 0))
             field[pair] = field[pair] + value
             wide[following, pair + 1, EDGE : EDGE + ROWS, :] = value.astype(BF)
+            if pair == QUADS[0][1]:
+                halo_begin(edge_halo(following))
+                halo_begin(core_halo(following))
+        halo_begin(middle_halo(following))
 
     field[...] = jnp.zeros(field.shape, F32)
     for pair in range(PAIRS):
@@ -587,8 +591,6 @@
             bound_end(2)
             coarse_solve()
             prolong(parity)
-            for halo in (middle_halo, edge_halo, core_halo):
-                halo_begin(halo(following))
 
         @pl.when(number == 5)
         def _():

time: 85.2 us -> 84.4 us (level)
  no operation moved by 1% of the time
where the time goes in v5:
time: 84.4 us; the launch traced here: 84 us
  Pallas kernels  83.9 us (99%)
    pallas_call x1, Pallas kernels, local(): pl.pallas_call(functools.partial(kernel, stream_total, span_total), out_s...  81.6 us
    pallas_call x1, Pallas kernels, local(): pl.pallas_call(unfold, out_shape=jax.ShapeDtypeStruct(right_side.shape, F...  2.26 us

profile of v5, /device:TPU:0, one launch (start us, length us, event | category | flops | bytes accessed | tf_op | source)
XLA Modules:
  0.0 84.0 jit_solution(12324543902888417584)
XLA Ops:
  0.0 81.6 %cycle.1.field_hbm = f32[4,512,128]{2,1,0:T(8,128)} custom-call(f32[8,4,64,128]{3,2,1,0:T(8,128)} %rhs_hbm.1, f32[8,64,128]{2,1,0:T(8,128)} %shift_hbm.1, bf16[8,64,64,128]{3,2,1,0:T(8,128)(2,1)} %diag_hbm.1, bf16[8,64,64,128]{3,2,1,0:T(8,128)(2,1)} %smooth_hbm.1, bf16[8,64,64]{2,1,0:T(8,128)(2,1)} %couple_hbm.1, f32[8,8,128]{2,1,0:T(8,128)} %coef_hbm.1, ...), custom_call_target="tpu_custom_call" | custom-call | tf_op jit(solution)/shard_map/cycle/pallas_call | solution.py:675
  81.6 2.3 %unfold.1 = f32[8,4,64,128]{3,2,1,0:T(8,128)} custom-call(f32[4,512,128]{2,1,0:T(8,128)} %cycle.1.field_hbm), custom_call_target="tpu_custom_call" | custom-call | tf_op jit(solution)/shard_map/unfold/pallas_call | solution.py:687
